TPU v7x, 32 devices: a whole 2x2x4 slice. The times are simulated.
32 devices in a mesh: sec: 2 (over core), tile: 16 (over z, y, x).
Axes of the slice: x: 2, y: 2, z: 4, core: 2. Of those that a mesh axis runs over, the one named last changes fastest.
Arguments:
- land_wind: float32 [4096, 128], P(('sec', 'tile')), may hold values from 0.15 to 0.9
- land_moist: float32 [4096, 128], P(('sec', 'tile')), may hold values from 0 to 0.3
- texture: int32 [4096, 128], P(('sec', 'tile')), may hold values from 0 to 3
- land_index: int32 [4096, 128], P(('sec', 'tile')), may hold values from 0 to 32767
- erod_map: float32 [1048576], P(('sec', 'tile')), may hold values from 0.2 to 1
- mass_frac: float32 [4, 12], replicated, may hold values from 0.02 to 0.3
- blast_table: float32 [4, 8, 12], replicated, may hold values from 0.05 to 1
- dest_tile: int32 [4096, 1], P(('sec', 'tile')), may hold values from 0 to 31; in each aligned block of 128 rows (0 to 127, 128 to 255, ...) at most 8 rows name the same one
- regrid_w: bfloat16 [4096, 128, 256], P(('sec', 'tile')), may hold values from 0 to 0.25, as said below
- atm_state: float32 [3, 16, 8192], P(None, None, ('sec', 'tile')), may hold values from -5 to 5
- dust_mix: float32 [8, 16, 8192], P(None, None, ('sec', 'tile')), may hold values from 0 to 1
- mixing: float32 [15, 8192], P(None, ('sec', 'tile')), may hold values from 0.1 to 10
- settle: float32 [8], replicated, may hold values from 0.05 to 0.5
Outputs:
- land_fields: float32 [2, 4096, 128], P(None, ('sec', 'tile'))
- dust_out: float32 [8, 16, 8192], P(None, None, ('sec', 'tile'))
Inputs may be any that keep to these rules, and one draw needn't show every extreme that they name: `land_index`: each land cell's index points into its own device's 32768 cells of erod_map. `dest_tile`: among the 128 blocks of one device at most 8 name the same tile, a bound that some block reaches. `regrid_w`: each land cell has 1 to 4 positive weights, of 0.05 or more, on adjacent columns of its tile, and 0 elsewhere.
All inputs are finite; a program needn't handle non-finite values.
Results may differ from a plain program's by a relative error of at most 0.0023.
Values may be sent and summed in bfloat16 or wider, within the bound.
A program may use at most 64 MiB of HBM per device.

v0:
```python
import jax
import jax.numpy as jnp
from jax import lax
from jax.sharding import PartitionSpec as P


def threshold_table(count):
    diameter = 4e-05 * jnp.power(jnp.float32(1.35), jnp.arange(count).astype(jnp.float32))
    return jnp.sqrt(0.0123 * (2160.0 * 9.81 * diameter + 0.0003 / (1.227 * diameter)))


def emit(wind_rows, moist_rows, texture_rows, erodible, mass_frac, blast_table, base_thresh):
    high = lax.Precision.HIGHEST
    thresh = base_thresh[:, None, None] * jnp.sqrt(1.0 + 12.1 * moist_rows)[None]
    classes = jnp.arange(mass_frac.shape[0])
    onehot = (texture_rows[None] == classes[:, None, None]).astype(jnp.float32)
    fraction = jnp.einsum("tb,tnl->bnl", mass_frac, onehot, precision=high)
    speed = wind_rows[None]
    salt = (
        40.0
        * fraction
        * erodible[None]
        * (speed + thresh)
        * jnp.maximum(speed * speed - thresh * thresh, 0.0)
    )
    blasted = jnp.einsum("tkb,bnl->tknl", blast_table, salt, precision=high)
    emission = jnp.sum(blasted * onehot[:, None], axis=0)
    return jnp.transpose(emission, (1, 0, 2)).astype(jnp.bfloat16)


def solve(right_side, coupling, sinking):
    levels = right_side.shape[1]
    sink_col = sinking[:, None]
    zero_row = jnp.zeros_like(coupling[0])
    ratios = []
    partial_value = []
    ratio_prev = None
    part_prev = None
    for level in range(levels):
        lower_c = coupling[level - 1] if level > 0 else zero_row
        upper_c = coupling[level] if level < levels - 1 else zero_row
        diagonal = 1.0 + lower_c[None] + upper_c[None] + sink_col
        if level == 0:
            pivot = diagonal
            part_now = right_side[:, level] / pivot
        else:
            pivot = diagonal + lower_c[None] * ratio_prev
            part_now = (right_side[:, level] + lower_c[None] * part_prev) / pivot
        if level < levels - 1:
            ratio_now = -(upper_c[None] + sink_col) / pivot
        else:
            ratio_now = jnp.zeros_like(pivot)
        ratios.append(ratio_now)
        partial_value.append(part_now)
        ratio_prev = ratio_now
        part_prev = part_now
    result = [None] * levels
    result[levels - 1] = partial_value[levels - 1]
    for level in range(levels - 2, -1, -1):
        result[level] = partial_value[level] - ratios[level] * result[level + 1]
    return jnp.stack(result, axis=1)


def on_device(
    land_wind,
    land_moist,
    texture,
    land_index,
    erod_map,
    mass_frac,
    blast_table,
    dest_tile,
    regrid_w,
    atm_state,
    dust_mix,
    mixing,
    settle,
):
    high = lax.Precision.HIGHEST
    nblocks, ncells = land_wind.shape
    columns = atm_state.shape[2]
    nbins = blast_table.shape[1]
    devices = lax.axis_size(("sec", "tile"))
    state = solve(atm_state, mixing, jnp.zeros((3,), jnp.float32))
    speed = jnp.sqrt(state[0, 0] ** 2 + state[1, 0] ** 2 + 0.25)
    surface = jnp.stack([speed, state[2, 0]]).astype(jnp.bfloat16).reshape(1, 2 * columns)
    gathered = lax.all_gather(surface, ("sec", "tile"), axis=0, tiled=True)
    base_thresh = threshold_table(mass_frac.shape[1])
    erodible = erod_map[land_index]
    emission = emit(land_wind, land_moist, texture, erodible, mass_frac, blast_table, base_thresh)
    partial_flux = jnp.einsum(
        "gkl,gla->gka", emission, regrid_w, preferred_element_type=jnp.float32
    )
    flat_flux = partial_flux.reshape(nblocks, nbins * columns)
    targets = dest_tile[:, 0]
    onehot = (targets[:, None] == jnp.arange(devices)[None, :]).astype(jnp.float32)
    capacity = max(2, 2 * nblocks // devices)
    before = jnp.cumsum(onehot, axis=0) - onehot
    ranking = jnp.sum(before * onehot, axis=1).astype(jnp.int32)
    slot_of = targets * capacity + ranking
    placing = (jnp.arange(devices * capacity)[:, None] == slot_of[None, :]).astype(jnp.float32)
    outgoing = jnp.dot(placing, flat_flux, precision=high).reshape(
        devices, capacity * nbins * columns
    )
    incoming = lax.all_to_all(
        outgoing.astype(jnp.bfloat16), ("sec", "tile"), split_axis=0, concat_axis=0, tiled=True
    ).astype(outgoing.dtype)
    flux = jnp.sum(incoming.reshape(devices * capacity, nbins, columns), axis=0)
    flux = flux * (float(columns) / float(ncells * nblocks))
    loaded = dust_mix.at[:, 0, :].add(flux)
    dust_out = solve(loaded, mixing, settle)
    picked = jnp.dot(onehot.astype(jnp.bfloat16), gathered, preferred_element_type=jnp.float32)
    picked = picked.astype(jnp.bfloat16).reshape(nblocks, 2, columns)
    numer = jnp.einsum("gla,gka->kgl", regrid_w, picked, preferred_element_type=jnp.float32)
    denom = jnp.sum(regrid_w, axis=2, dtype=jnp.float32)
    land_fields = jnp.stack([numer[0] / denom, 0.5 * land_moist + 0.5 * numer[1] / denom])
    return (land_fields, dust_out)


def solution(mesh):
    in_specs = (
        P(("sec", "tile"), None),
        P(("sec", "tile"), None),
        P(("sec", "tile"), None),
        P(("sec", "tile"), None),
        P(("sec", "tile")),
        P(),
        P(),
        P(("sec", "tile"), None),
        P(("sec", "tile"), None, None),
        P(None, None, ("sec", "tile")),
        P(None, None, ("sec", "tile")),
        P(None, ("sec", "tile")),
        P(),
    )
    out_specs = (P(None, ("sec", "tile"), None), P(None, None, ("sec", "tile")))
    return jax.shard_map(
        on_device, mesh=mesh, in_specs=in_specs, out_specs=out_specs, check_vma=False
    )
```

profile of v0, /device:TPU:0, one launch (start us, length us, event | category | flops | bytes accessed | tf_op | source)
XLA Modules:
  0.0 240.3 jit_solution(10112823659823847269)
XLA Ops:
  0.6 1.0 fusion.78
  1.7 1.0 broadcast_add_fusion.1
  2.7 0.9 fusion.79
  3.6 1.2 fusion.77
  4.9 0.1 multiply_add_fusion.15
  5.1 0.1 multiply_subtract_fusion.14
  5.4 70.3 %all-gather = bf16[32,1,512]{2,1,0:T(2,128)(2,1)S(1)} all-gather(bf16[1,1,512]{2,1,0:T(2,128)(2,1)S(1)} %reshape.27177), channel_id=1, replica_groups=mesh['sec'=2,'tile'=16] {'sec','tile'}, dimensions={0}, use_global_device_ids=true | all-gather | bytes 33792 | tf_op jit(solution)/shard_map/all_gather | solution.py:87
  75.6 0.7 fusion.15
  76.4 0.9 convolution_convert_fusion.1
  77.3 5.8 %convert_reduce_fusion = f32[128,128]{1,0:T(8,128)S(1)} fusion(bf16[128,128,256]{2,1,0:T(8,128)(2,1)} %param.23), kind=kLoop, calls=%fused_computation.1 | loop fusion | flops 8372224 | bytes 8454144 | tf_op jit(solution)/shard_map/reduce_sum | solution.py:115
  83.1 2.3 convolution_bitcast_fusion
  85.4 0.1 fusion.76
  85.6 90.5 %gather_fusion = f32[16384]{0:T(1024)S(1)} fusion(f32[32768]{0:T(1024)S(1)} %copy-done, s32[16384]{0:T(1024)S(1)} %fusion.13), kind=kCustom, calls=%fused_computation | custom fusion | bytes 196608 | tf_op jit(solution)/shard_map/gather | solution.py:89
  176.2 0.1 fusion.10
  176.3 0.8 fusion.4
  177.2 1.9 fusion
  179.1 4.6 %fusion.7 = f32[128,8,256]{2,1,0:T(8,128)S(1)} fusion(bf16[128,128,256]{2,1,0:T(8,128)(2,1)} %param.23, bf16[8,128,128]{2,0,1:T(8,128)(2,1)S(1)} %fusion), kind=kOutput, calls=%fused_computation.17 | convolution fusion | flops 67108864 | bytes 9699328 | tf_op jit(solution)/shard_map/gkl,gla->gka/dot_general | solution.py:91
  183.6 0.3 copy.136
  184.0 0.2 reduce_window_sum.11
  184.2 0.1 copy-done.31
  184.3 0.2 select_reduce_fusion
  184.5 1.0 convolution_convert_fusion
  185.5 1.9 convert_element_type.86
  187.4 0.5 broadcast.18933
  187.9 7.1 %reduce.4 = bf16[32,16384]{1,0:T(8,128)(2,1)S(1)} reduce(bf16[32,1,16384]{2,1,0:T(2,128)(2,1)S(1)} %convert_element_type.86, bf16[]{:T(256)} %broadcast.18933), dimensions={1}, to_apply=%convert_element_type.86.reduce_sub_computation | reduce | bytes 2097154 | tf_op jit(solution)/shard_map/convert_element_type | solution.py:106
  195.0 1.6 reshape.27184
  196.6 2.9 %all-to-all-start = ((bf16[32,2,8192]{2,1,0:T(2,128)(2,1)}), bf16[32,2,8192]{2,1,0:T(2,128)(2,1)S(1)}, u32[]{:S(2)}, u32[]{:S(2)}) async-start(bf16[32,2,8192]{2,1,0:T(2,128)(2,1)} %reshape.27184), calls=%async_computation | async-start | bytes 2097152 | tf_op jit(solution)/shard_map/all_to_all | solution.py:105
  199.5 0.7 pad_maximum_fusion
  200.2 0.1 fusion.75
  200.3 27.1 %all-to-all-done = bf16[32,2,8192]{2,1,0:T(2,128)(2,1)S(1)} async-done(((bf16[32,2,8192]{2,1,0:T(2,128)(2,1)}), bf16[32,2,8192]{2,1,0:T(2,128)(2,1)S(1)}, u32[]{:S(2)}, u32[]{:S(2)}) %all-to-all-start) | async-done | bytes 1048608 | tf_op jit(solution)/shard_map/all_to_all | solution.py:105
  227.3 1.0 reshape.27185
  228.4 7.4 %convert_reduce_fusion.1 = f32[32,16384]{1,0:T(8,128)} fusion(bf16[32,1,16384]{2,1,0:T(2,128)(2,1)S(1)} %reshape.27185), kind=kLoop, calls=%fused_computation.5 | loop fusion | flops 524288 | bytes 3145728 | tf_op jit(solution)/shard_map/convert_element_type | solution.py:107
  235.8 1.7 reshape.27164
  237.7 0.3 reduce_sum.42
  237.9 0.3 copy-done.7
  238.2 0.0 copy-done.9
  238.2 0.0 copy-done.11
  238.2 0.0 copy-done.23
  238.3 0.2 fusion.28
  238.5 0.2 constant_dynamic-update-slice_fusion.15
  238.7 0.1 constant_dynamic-update-slice_fusion.14
  238.8 0.1 constant_dynamic-update-slice_fusion.11
  238.9 0.1 constant_dynamic-update-slice_fusion.9
  239.1 0.1 constant_dynamic-update-slice_fusion.5
  239.2 0.1 constant_dynamic-update-slice_fusion.3
  239.3 0.1 constant_dynamic-update-slice_fusion.1
  239.4 0.1 constant_dynamic-update-slice_fusion
  239.6 0.7 copy.100
  (81 shorter events, 0.4 us)
Async XLA Ops:
  0.6 84.9 %copy-start = (f32[32768]{0:T(1024)S(1)}, f32[32768]{0:T(1024)}, u32[]{:S(2)}) copy-start(f32[32768]{0:T(1024)} %param.19) | copy-start | bytes 393220
  1.6 3.4 %copy-start.14 = (f32[1,256]{1,0:T(1,128)}, f32[1,256]{1,0:T(1,128)S(1)}, u32[]{:S(2)}) copy-start(f32[1,256]{1,0:T(1,128)S(1)} %get-tuple-element.113) | copy-start | bytes 3076
  1.6 3.4 %copy-start.16 = (f32[1,256]{1,0:T(1,128)}, f32[1,256]{1,0:T(1,128)S(1)}, u32[]{:S(2)}) copy-start(f32[1,256]{1,0:T(1,128)S(1)} %get-tuple-element.114) | copy-start | bytes 3076
  1.6 3.4 %copy-start.18 = (f32[1,256]{1,0:T(1,128)}, f32[1,256]{1,0:T(1,128)S(1)}, u32[]{:S(2)}) copy-start(f32[1,256]{1,0:T(1,128)S(1)} %get-tuple-element.115) | copy-start | bytes 3076
  1.7 3.5 %copy-start.24 = (f32[1,256]{1,0:T(1,128)}, f32[1,256]{1,0:T(1,128)S(1)}, u32[]{:S(2)}) copy-start(f32[1,256]{1,0:T(1,128)S(1)} %get-tuple-element.121) | copy-start | bytes 3076
  2.7 2.2 copy-start.8
  2.7 2.4 copy-start.10
  2.7 2.4 copy-start.12
  2.7 2.4 copy-start.20
  2.7 2.4 copy-start.22
  2.7 2.5 %copy-start.27 = (f32[1,256]{1,0:T(1,128)}, f32[1,256]{1,0:T(1,128)S(1)}, u32[]{:S(2)}) copy-start(f32[1,256]{1,0:T(1,128)S(1)} %get-tuple-element.106) | copy-start | bytes 3076
  2.7 2.6 %copy-start.29 = (f32[1,256]{1,0:T(1,128)}, f32[1,256]{1,0:T(1,128)S(1)}, u32[]{:S(2)}) copy-start(f32[1,256]{1,0:T(1,128)S(1)} %get-tuple-element.107) | copy-start | bytes 3076
  77.3 5.8 %copy-start.1 = (bf16[128,128,256]{2,1,0:T(8,128)(2,1)S(1)}, bf16[128,128,256]{2,1,0:T(8,128)(2,1)}, u32[]{:S(2)}) copy-start(bf16[128,128,256]{2,1,0:T(8,128)(2,1)} %param.23) | copy-start | bytes 25165828
  83.1 2.4 copy-start.6
  85.5 90.6 %copy-start.2 = (f32[128,128]{1,0:T(8,128)S(1)}, f32[128,128]{1,0:T(8,128)}, u32[]{:S(2)}) copy-start(f32[128,128]{1,0:T(8,128)} %param.15) | copy-start | bytes 196612
  85.6 90.6 %copy-start.5 = (s32[128,128]{1,0:T(8,128)S(1)}, s32[128,128]{1,0:T(8,128)}, u32[]{:S(2)}) copy-start(s32[128,128]{1,0:T(8,128)} %param.17) | copy-start | bytes 196612
  85.6 90.7 %copy-start.4 = (f32[128,128]{1,0:T(8,128)S(1)}, f32[128,128]{1,0:T(8,128)}, u32[]{:S(2)}) copy-start(f32[128,128]{1,0:T(8,128)} %param.16) | copy-start | bytes 196612
  85.6 90.7 %copy-start.32 = (f32[4,12]{1,0:T(4,128)S(1)}, f32[4,12]{1,0:T(4,128)}, u32[]{:S(2)}) copy-start(f32[4,12]{1,0:T(4,128)} %param.20) | copy-start | bytes 580
  176.1 1.0 copy-start.26
  183.6 0.7 copy-start.31
  195.0 5.2 %copy-start.3 = (f32[8,16,256]{2,1,0:T(8,128)S(1)}, f32[8,16,256]{2,1,0:T(8,128)}, u32[]{:S(2)}) copy-start(f32[8,16,256]{2,1,0:T(8,128)} %param.25) | copy-start | bytes 393220
  196.6 30.7 %all-to-all-start = ((bf16[32,2,8192]{2,1,0:T(2,128)(2,1)}), bf16[32,2,8192]{2,1,0:T(2,128)(2,1)S(1)}, u32[]{:S(2)}, u32[]{:S(2)}) async-start(bf16[32,2,8192]{2,1,0:T(2,128)(2,1)} %reshape.27184), calls=%async_computation | async-start | bytes 2097152 | tf_op jit(solution)/shard_map/all_to_all | solution.py:105
  237.5 0.7 copy-start.7
  237.5 0.7 copy-start.9
  237.6 0.7 copy-start.11
  237.6 0.7 copy-start.13
  237.6 0.7 copy-start.21
  237.6 0.7 copy-start.23
  237.6 0.7 copy-start.25
  237.6 0.7 copy-start.28
  237.6 0.7 copy-start.30
  237.6 0.8 copy-start.15
  237.6 0.8 copy-start.17
  237.6 0.8 copy-start.19
where the time goes:
time: 241 us; the launch traced here: 240 us
  local copies, waits for them, and re-layouts  101 us (42%)
  blocking collectives  70.3 us (29%)
  waiting for transfers between devices  27.1 us (11%)
  other arithmetic  26 us (11%)
  matrix products  11.4 us (5%)
  starting transfers between devices  2.86 us (1%)
    gather x1, local copies, waits for them, and re-layouts, on_device(): erodible = erod_map[land_index]  90.5 us
    all_gather x1, blocking collectives, on_device(): gathered = lax.all_gather(surface, ('sec', 'tile'), axis=0, tiled=True)  70.3 us
    all_to_all x1, waiting for transfers between devices, on_device(): lax.all_to_all(outgoing.astype(jnp.bfloat16), ('sec', 'tile'), split_axis...  27.1 us
    convert_element_type x1, other arithmetic, on_device(): incoming = lax.all_to_all(outgoing.astype(jnp.bfloat16), ('sec', 'tile'),...  7.42 us
    convert_element_type x1, other arithmetic, on_device(): outgoing.astype(jnp.bfloat16)  7.05 us
    reduce_sum x1, other arithmetic, on_device(): denom = jnp.sum(regrid_w, axis=2, dtype=jnp.float32)  5.77 us
  transfers between devices with their start and end apart: 1, of which 1 were waited for; matrix products, arithmetic and copies ran while one was open for 0% of the time, Pallas kernels for 0%

commit v1 on v0

v1 whole, which is shorter than its diff:
```python
import functools

import jax
import jax.numpy as jnp
import numpy as np
from jax import lax
from jax.experimental import pallas as pl
from jax.experimental.pallas import tpu as pltpu
from jax.sharding import PartitionSpec as P

MESH = pl.DeviceIdType.MESH
F32 = jnp.float32
BF16 = jnp.bfloat16
FIXED = 65535.0


def threshold_constants(count):
    diameter = 4e-05 * np.power(1.35, np.arange(count))
    return np.sqrt(0.0123 * (2160.0 * 9.81 * diameter + 0.0003 / (1.227 * diameter)))


def rows_of(values, shape):
    row = lax.broadcasted_iota(jnp.int32, shape, 0)
    total = jnp.zeros(shape, F32)
    for r, value in enumerate(values):
        total = jnp.where(row == r, value, total)
    return total


def kernel(
    n, nt, nblocks, ncells, columns, nbins, nsalt, ntex, levels,
    wind_hbm, moist_hbm, tex_hbm, index_hbm, map_hbm, frac_hbm, blast_hbm, dest_hbm,
    w_hbm, atm_hbm, dust_hbm, mix_hbm, settle_hbm,
    land_out, dust_out,
    wind, moist, tex, index, soil, frac, blast, dest_v, dest_s, w, atm, dust, mix, settle,
    packed, erod, root, coef, part, sums, send, came, mine, gath, numer, base, gain,
    in_sem, w_sem, surf_send, surf_recv, flux_send, flux_recv,
):
    half = columns // 2
    me = lax.axis_index("sec") * nt + lax.axis_index("tile")

    def local(src, dst, k):
        copy = pltpu.make_async_copy(src, dst, in_sem.at[k])
        copy.start()
        return copy

    c_mix = local(mix_hbm, mix, 0)
    c_atm = local(atm_hbm, atm, 1)
    c_map = local(map_hbm, soil, 2)
    c_index = local(index_hbm, index, 3)
    c_wind = local(wind_hbm, wind, 4)
    c_moist = local(moist_hbm, moist, 5)
    c_tex = local(tex_hbm, tex, 6)
    c_frac = local(frac_hbm, frac, 7)
    c_blast = local(blast_hbm, blast, 8)
    c_dv = local(dest_hbm, dest_v, 9)
    c_ds = local(dest_hbm, dest_s, 10)
    c_settle = local(settle_hbm, settle, 11)
    c_d0 = local(dust_hbm.at[:, 0:half], dust.at[0], 12)
    c_d1 = local(dust_hbm.at[:, half:columns], dust.at[1], 13)
    groups = nblocks // 8

    def chunk(i):
        at = pl.ds(i * 8, 8)
        return pltpu.make_async_copy(w_hbm.at[at], w.at[at], w_sem.at[i])

    def fetch(i, carry):
        chunk(i).start()
        return carry

    lax.fori_loop(0, groups, fetch, 0)

    def peer(i):
        p = lax.rem(me + i, n)
        return p, (p // nt, lax.rem(p, nt))

    barrier = pltpu.get_barrier_semaphore()

    def greet(i, carry):
        pl.semaphore_signal(barrier, inc=1, device_id=peer(i)[1], device_id_type=MESH)
        return carry

    lax.fori_loop(1, n, greet, 0)

    c_mix.wait()
    c_atm.wait()
    above = None
    held = [None] * 3
    for level in range(levels - 1, -1, -1):
        pivot = jnp.ones((1, columns), F32)
        low = up = None
        if level > 0:
            low = mix[level - 1:level, :]
            pivot = pivot + low
        if level < levels - 1:
            up = mix[level:level + 1, :]
            pivot = pivot + up * (1.0 - above)
        inverse = 1.0 / pivot
        for f in range(3):
            right = atm[f, level:level + 1, :]
            if up is not None:
                right = right + up * held[f]
            held[f] = right * inverse
        if low is not None:
            above = low * inverse
    speed = jnp.sqrt(held[0] * held[0] + held[1] * held[1] + 0.25)
    mine[0:1, :] = speed.astype(BF16).astype(F32)
    mine[1:2, :] = held[2].astype(BF16).astype(F32)

    c_map.wait()
    c_index.wait()
    words = soil.shape[0] // 2
    fixed = jnp.floor(soil[...] * FIXED + 0.5).astype(jnp.int32)
    packed[...] = fixed[:words] + (fixed[words:] << 16)
    bits = words.bit_length() - 1

    def erode(i, carry):
        at = pl.ds(pl.multiple_of(i * 8, 8), 8)
        cell = index[at, :]
        lane = cell & 127
        row = cell >> 7
        picks = [((row >> b) & 1) == 1 for b in range(bits)]

        def tree(bit, first):
            if bit < 0:
                words_row = jnp.broadcast_to(packed[first:first + 1, :], (8, 128))
                return jnp.take_along_axis(words_row, lane, axis=1, mode="promise_in_bounds")
            return jnp.where(picks[bit], tree(bit - 1, first + (1 << bit)), tree(bit - 1, first))

        word = tree(bits - 1, 0)
        value = jnp.where(row >= words, lax.shift_right_logical(word, 16), word) & 65535
        erod[at, :] = value.astype(F32) * (1.0 / FIXED)
        return carry

    lax.fori_loop(0, groups, erode, 0)

    pl.semaphore_wait(barrier, n - 1)

    def send_surface(i, carry):
        pltpu.make_async_remote_copy(
            src_ref=mine, dst_ref=gath.at[me], send_sem=surf_send, recv_sem=surf_recv,
            device_id=peer(i)[1], device_id_type=MESH,
        ).start()
        return carry

    lax.fori_loop(1, n, send_surface, 0)
    gath[me] = mine[...]

    c_frac.wait()
    c_blast.wait()
    coef[...] = jnp.zeros_like(coef)
    for t in range(ntex):
        coef[:, 16 * t:16 * t + nsalt] = 40.0 * blast[t] * frac[t:t + 1, :]
    full = coef[:, 0:16 * ntex]
    coarse = full.astype(BF16)
    fine = (full - coarse.astype(F32)).astype(BF16)
    table = jnp.concatenate([coarse, fine], axis=0)
    c_wind.wait()
    c_moist.wait()
    c_tex.wait()
    root[...] = jnp.sqrt(1.0 + 12.1 * moist[...])
    thresh0 = rows_of([float(v) for v in threshold_constants(nsalt)], (16, ncells))
    nothing = jnp.zeros((nbins, ncells), F32)

    def regrid(i, carry):
        chunk(i).wait()
        blocks = []
        for j in range(8):
            at = pl.ds(i * 8 + j, 1)
            speed_row = jnp.broadcast_to(wind[at, :], (16, ncells))
            thresh = thresh0 * jnp.broadcast_to(root[at, :], (16, ncells))
            total = speed_row + thresh
            salt = jnp.broadcast_to(erod[at, :], (16, ncells)) * total * (
                total * jnp.maximum(speed_row - thresh, 0.0)
            )
            kind = jnp.broadcast_to(tex[at, :], (16, ncells))
            blocks.append(
                jnp.concatenate(
                    [jnp.where(kind == t, salt, 0.0).astype(BF16) for t in range(ntex)], axis=0
                )
            )
        both = jnp.dot(table, jnp.concatenate(blocks, axis=1), preferred_element_type=F32)
        emission = both[0:nbins] + both[nbins:2 * nbins]
        for j in range(0, 8, 2):
            first = emission[:, j * ncells:(j + 1) * ncells]
            second = emission[:, (j + 1) * ncells:(j + 2) * ncells]
            left = jnp.concatenate(
                [
                    jnp.concatenate([first, nothing], axis=1),
                    jnp.concatenate([nothing, second], axis=1),
                ],
                axis=0,
            ).astype(BF16)
            weights = w[pl.ds(i * 8 + j, 2)].reshape(2 * ncells, columns)
            flux = jnp.dot(left, weights, preferred_element_type=F32)
            for s in range(2):
                at = pl.ds(i * 8 + j + s, nbins, stride=nblocks)
                part[0, at, :] = flux[s * nbins:(s + 1) * nbins, 0:half]
                part[1, at, :] = flux[s * nbins:(s + 1) * nbins, half:columns]
        return carry

    lax.fori_loop(0, groups, regrid, 0)

    c_dv.wait()
    tiles = lax.broadcasted_iota(jnp.int32, (n, nblocks), 0)
    placing = jnp.where(jnp.broadcast_to(dest_v[...], (n, nblocks)) == tiles, 1.0, 0.0).astype(BF16)
    placing = jnp.concatenate([placing, placing], axis=1)
    for k in range(nbins):
        at = slice(k * nblocks, (k + 1) * nblocks)
        block = jnp.concatenate([part[0, at, :], part[1, at, :]], axis=1)
        high = block.astype(BF16)
        low = (block - high.astype(F32)).astype(BF16)
        total = jnp.dot(placing, jnp.concatenate([high, low], axis=0), preferred_element_type=F32)
        sums[pl.ds(k, n, stride=2 * nbins), :] = total[:, 0:half]
        sums[pl.ds(nbins + k, n, stride=2 * nbins), :] = total[:, half:columns]
    send[...] = sums[...].reshape(n, 2 * nbins, half).astype(BF16)

    def send_flux(i, carry):
        p, target = peer(i)
        pltpu.make_async_remote_copy(
            src_ref=send.at[p], dst_ref=came.at[me], send_sem=flux_send, recv_sem=flux_recv,
            device_id=target, device_id_type=MESH,
        ).start()
        return carry

    lax.fori_loop(1, n, send_flux, 0)
    came[me] = send[me]

    c_settle.wait()
    c_d0.wait()
    c_d1.wait()
    sink = rows_of([settle[0, f] for f in range(nbins)], (nbins, columns))
    ratios = [None] * levels
    values = [None] * levels
    for level in range(levels - 1, -1, -1):
        pivot = jnp.ones((nbins, columns), F32)
        at = pl.ds(level, nbins, stride=levels)
        right = jnp.concatenate([dust[0, at, :], dust[1, at, :]], axis=1)
        low = None
        if level > 0:
            low = jnp.broadcast_to(mix[level - 1:level, :], (nbins, columns))
            pivot = pivot + low
        if level < levels - 1:
            up = jnp.broadcast_to(mix[level:level + 1, :], (nbins, columns)) + sink
            pivot = pivot + up * (1.0 - ratios[level + 1])
            right = right + up * values[level + 1]
        else:
            pivot = pivot + sink
        inverse = 1.0 / pivot
        values[level] = right * inverse
        if low is not None:
            ratios[level] = low * inverse
    scale = float(columns) / float(ncells * nblocks)
    now, step = values[0], inverse * scale
    base[0], gain[0] = now, step
    for level in range(1, levels):
        now = values[level] + ratios[level] * now
        step = ratios[level] * step
        base[level], gain[level] = now, step

    c_ds.wait()
    arrived = gath.at[pl.ds(0, n - 1)]
    pltpu.make_async_copy(arrived, arrived, surf_recv).wait()
    rest = jnp.where(lax.broadcasted_iota(jnp.int32, (6, columns), 0) == 0, 1.0, 0.0)

    def back(i, carry):
        for j in range(0, 8, 2):
            g = i * 8 + j
            left = jnp.concatenate(
                [gath[dest_s[0, g]], rest, gath[dest_s[0, g + 1]], rest], axis=0
            ).astype(BF16)
            weights = w[pl.ds(g, 2)].reshape(2 * ncells, columns)
            found = lax.dot_general(
                left, weights, (((1,), (1,)), ((), ())), preferred_element_type=F32
            )
            numer[pl.ds(pl.multiple_of(g * 8, 8), 8), :] = found[0:8, 0:ncells]
            numer[pl.ds(pl.multiple_of(g * 8 + 8, 8), 8), :] = found[8:16, ncells:2 * ncells]
        return carry

    lax.fori_loop(0, groups, back, 0)
    weight = 1.0 / numer[pl.ds(2, nblocks, stride=8), :]
    land_out[0] = numer[pl.ds(0, nblocks, stride=8), :] * weight
    land_out[1] = 0.5 * moist[...] + 0.5 * (numer[pl.ds(1, nblocks, stride=8), :] * weight)

    landed = came.at[pl.ds(0, n - 1)]
    pltpu.make_async_copy(landed, landed, flux_recv).wait()
    flux = jnp.sum(came[...].astype(F32), axis=0)
    flux = jnp.concatenate([flux[0:nbins], flux[nbins:2 * nbins]], axis=1)
    for level in range(levels):
        dust_out[:, level, :] = base[level] + gain[level] * flux

    sent = gath.at[pl.ds(0, n - 1)]
    pltpu.make_async_copy(sent, sent, surf_send).wait()
    gone = came.at[pl.ds(0, n - 1)]
    pltpu.make_async_copy(gone, gone, flux_send).wait()


def on_device(
    nt, land_wind, land_moist, texture, land_index, erod_map, mass_frac, blast_table, dest_tile,
    regrid_w, atm_state, dust_mix, mixing, settle,
):
    nblocks, ncells = land_wind.shape
    columns = regrid_w.shape[2]
    ntex, nbins, nsalt = blast_table.shape
    levels = atm_state.shape[1]
    half = columns // 2
    n = lax.axis_size(("sec", "tile"))
    groups = nblocks // 8
    soil = erod_map.reshape(-1, 128)
    land = pltpu.VMEM((nblocks, ncells), F32)
    whole = pltpu.VMEM((nblocks, ncells), jnp.int32)
    return pl.pallas_call(
        functools.partial(kernel, n, nt, nblocks, ncells, columns, nbins, nsalt, ntex, levels),
        out_shape=(
            jax.ShapeDtypeStruct((2, nblocks, ncells), F32),
            jax.ShapeDtypeStruct((nbins, levels, columns), F32),
        ),
        in_specs=[pl.BlockSpec(memory_space=pl.ANY)] * 13,
        out_specs=(pl.BlockSpec(memory_space=pltpu.VMEM), pl.BlockSpec(memory_space=pltpu.VMEM)),
        scratch_shapes=[
            land,
            land,
            whole,
            whole,
            pltpu.VMEM(soil.shape, F32),
            pltpu.VMEM(mass_frac.shape, F32),
            pltpu.VMEM(blast_table.shape, F32),
            pltpu.VMEM((1, nblocks), jnp.int32),
            pltpu.SMEM((1, nblocks), jnp.int32),
            pltpu.VMEM(regrid_w.shape, BF16),
            pltpu.VMEM(atm_state.shape, F32),
            pltpu.VMEM((2, nbins * levels, half), F32),
            pltpu.VMEM(mixing.shape, F32),
            pltpu.SMEM((1, nbins), F32),
            pltpu.VMEM((soil.shape[0] // 2, 128), jnp.int32),
            land,
            land,
            pltpu.VMEM((nbins, 128), F32),
            pltpu.VMEM((2, nbins * nblocks, half), F32),
            pltpu.VMEM((n * 2 * nbins, half), F32),
            pltpu.VMEM((n, 2 * nbins, half), BF16),
            pltpu.VMEM((n, 2 * nbins, half), BF16),
            pltpu.VMEM((2, columns), F32),
            pltpu.VMEM((n, 2, columns), F32),
            pltpu.VMEM((nblocks * 8, ncells), F32),
            pltpu.VMEM((levels, nbins, columns), F32),
            pltpu.VMEM((levels, nbins, columns), F32),
            pltpu.SemaphoreType.DMA((14,)),
            pltpu.SemaphoreType.DMA((groups,)),
            pltpu.SemaphoreType.DMA,
            pltpu.SemaphoreType.DMA,
            pltpu.SemaphoreType.DMA,
            pltpu.SemaphoreType.DMA,
        ],
        compiler_params=pltpu.CompilerParams(
            collective_id=0, has_side_effects=True, vmem_limit_bytes=40 * 1024 * 1024
        ),
    )(
        land_wind, land_moist, texture, land_index, soil, mass_frac, blast_table,
        dest_tile.reshape(1, nblocks), regrid_w, atm_state,
        dust_mix.reshape(nbins * levels, columns), mixing, settle.reshape(1, nbins),
    )


def solution(mesh):
    both = ("sec", "tile")
    in_specs = (
        P(both, None),
        P(both, None),
        P(both, None),
        P(both, None),
        P(both),
        P(),
        P(),
        P(both, None),
        P(both, None, None),
        P(None, None, both),
        P(None, None, both),
        P(None, both),
        P(),
    )
    out_specs = (P(None, both, None), P(None, None, both))
    return jax.shard_map(
        functools.partial(on_device, mesh.shape["tile"]),
        mesh=mesh, in_specs=in_specs, out_specs=out_specs, check_vma=False,
    )
```

time: 241 us -> 36.5 us (0.15)
  local copies, waits for them, and re-layouts: 101 us -> 14.1 us
  blocking collectives: 70.3 us -> 0 us
  waiting for transfers between devices: 27.1 us -> 0 us
  other arithmetic: 26 us -> 0 us
  Pallas kernels: 0 us -> 21.2 us
  matrix products: 11.4 us -> 0 us
  starting transfers between devices: 2.86 us -> 0 us
    gather x1 -> x0, local copies, waits for them, and re-layouts: 90.5 us -> none  [on_device(): erodible = erod_map[land_index]]
    all_gather x1 -> x0, blocking collectives: 70.3 us -> none  [on_device(): gathered = lax.all_gather(surface, ('sec', 'tile'), axis=0, tiled=True)]
    all_to_all x1 -> x0, waiting for transfers between devices: 27.1 us -> none  [on_device(): lax.all_to_all(outgoing.astype(jnp.bfloat16), ('sec', 'tile'), split_axis...]
    pallas_call x0 -> x1, Pallas kernels: none -> 21.2 us  [on_device(): pl.pallas_call(functools.partial(kernel, n, nt, nblocks, ncells, columns,...]
    convert_element_type x4 -> x0, other arithmetic: 15.3 us -> none  [the longest x1 7.42 us: on_device(): incoming = lax.all_to_all(outgoing.astype(jnp.bfloat16), ('sec', 'tile'),...]
    dot_general x6 -> x0, matrix products: 11.4 us -> none  [the longest x1 4.57 us: on_device(): jnp.einsum('gkl,gla->gka', emission, regrid_w, preferred_element_type=jnp...]
    unnamed x78 -> x28, local copies, waits for them, and re-layouts: 4.36 us -> 14.1 us
    reduce_sum x3 -> x0, other arithmetic: 6.21 us -> none  [the longest x1 5.77 us: on_device(): denom = jnp.sum(regrid_w, axis=2, dtype=jnp.float32)]
  transfers between devices with their start and end apart: 1 -> 0, of which waited for: 1 -> 0; matrix products, arithmetic and copies ran while one was open for 0% -> 0% of each run, Pallas kernels for 0% -> 0%
where the time goes in v1:
time: 36.5 us; the launch traced here: 35.9 us
  Pallas kernels  21.2 us (58%)
  local copies, waits for them, and re-layouts  14.1 us (39%)
  between operations  0.66 us (2%)
    pallas_call x1, Pallas kernels, on_device(): pl.pallas_call(functools.partial(kernel, n, nt, nblocks, ncells, columns,...  21.2 us
    unnamed x28, local copies, waits for them, and re-layouts  14.1 us

profile of v1, /device:TPU:0, one launch (start us, length us, event | category | flops | bytes accessed | tf_op | source)
XLA Modules:
  0.0 35.9 jit_solution(13177835753788312685)
XLA Ops:
  0.6 0.0 copy-start
  0.6 3.4 %copy-done = bf16[128,128,256]{2,1,0:T(8,128)(2,1)S(1)} copy-done((bf16[128,128,256]{2,1,0:T(8,128)(2,1)S(1)}, bf16[128,128,256]{2,1,0:T(8,128)(2,1)}, u32[]{:S(2)}) %copy-start) | copy-done | bytes 8388632
  4.0 0.0 copy-start.1
  4.0 0.9 %copy-done.1 = f32[32768]{0:T(1024)S(1)} copy-done((f32[32768]{0:T(1024)S(1)}, f32[32768]{0:T(1024)}, u32[]{:S(2)}) %copy-start.1) | copy-done | bytes 131096
  4.9 0.0 copy-start.2
  4.9 0.9 %copy-done.2 = f32[8,16,256]{2,1,0:T(8,128)S(1)} copy-done((f32[8,16,256]{2,1,0:T(8,128)S(1)}, f32[8,16,256]{2,1,0:T(8,128)}, u32[]{:S(2)}) %copy-start.2) | copy-done | bytes 131096
  5.8 0.0 copy-start.3
  5.8 0.8 %copy-done.3 = f32[128,128]{1,0:T(8,128)S(1)} copy-done((f32[128,128]{1,0:T(8,128)S(1)}, f32[128,128]{1,0:T(8,128)}, u32[]{:S(2)}) %copy-start.3) | copy-done | bytes 65560
  6.7 0.0 copy-start.4
  6.7 0.8 %copy-done.4 = f32[128,128]{1,0:T(8,128)S(1)} copy-done((f32[128,128]{1,0:T(8,128)S(1)}, f32[128,128]{1,0:T(8,128)}, u32[]{:S(2)}) %copy-start.4) | copy-done | bytes 65560
  7.5 0.0 copy-start.5
  7.5 0.8 %copy-done.5 = s32[128,128]{1,0:T(8,128)S(1)} copy-done((s32[128,128]{1,0:T(8,128)S(1)}, s32[128,128]{1,0:T(8,128)}, u32[]{:S(2)}) %copy-start.5) | copy-done | bytes 65560
  8.3 0.0 copy-start.6
  8.3 0.8 %copy-done.6 = s32[128,128]{1,0:T(8,128)S(1)} copy-done((s32[128,128]{1,0:T(8,128)S(1)}, s32[128,128]{1,0:T(8,128)}, u32[]{:S(2)}) %copy-start.6) | copy-done | bytes 65560
  9.2 0.0 copy-start.7
  9.2 0.8 %copy-done.7 = f32[3,16,256]{2,1,0:T(8,128)S(1)} copy-done((f32[3,16,256]{2,1,0:T(8,128)S(1)}, f32[3,16,256]{2,1,0:T(8,128)}, u32[]{:S(2)}) %copy-start.7) | copy-done | bytes 49176
  10.0 0.0 copy-start.8
  10.0 0.7 %copy-done.8 = f32[4,8,12]{2,1,0:T(8,128)S(1)} copy-done((f32[4,8,12]{2,1,0:T(8,128)S(1)}, f32[4,8,12]{2,1,0:T(8,128)}, u32[]{:S(2)}) %copy-start.8) | copy-done | bytes 1560
  10.7 0.0 copy-start.9
  10.7 0.7 %copy-done.9 = f32[15,256]{1,0:T(8,128)S(1)} copy-done((f32[15,256]{1,0:T(8,128)S(1)}, f32[15,256]{1,0:T(8,128)}, u32[]{:S(2)}) %copy-start.9) | copy-done | bytes 15384
  11.4 0.0 copy-start.10
  11.4 0.7 %copy-done.10 = f32[4,12]{1,0:T(4,128)S(1)} copy-done((f32[4,12]{1,0:T(4,128)S(1)}, f32[4,12]{1,0:T(4,128)}, u32[]{:S(2)}) %copy-start.10) | copy-done | bytes 216
  12.1 0.0 copy-start.11
  12.1 0.7 %copy-done.11 = s32[128,1]{0,1:T(1,128)S(1)} copy-done((s32[128,1]{0,1:T(1,128)S(1)}, s32[128,1]{0,1:T(1,128)}, u32[]{:S(2)}) %copy-start.11) | copy-done | bytes 536
  12.8 0.0 copy-start.12
  12.8 0.7 %copy-done.12 = f32[8]{0:T(128)S(1)} copy-done((f32[8]{0:T(128)S(1)}, f32[8]{0:T(128)}, u32[]{:S(2)}) %copy-start.12) | copy-done | bytes 56
  13.4 21.2 %shard_map.140 = (f32[2,128,128]{2,1,0:T(8,128)S(1)}, f32[8,16,256]{2,1,0:T(8,128)S(1)}) custom-call(f32[128,128]{1,0:T(8,128)S(1)} %copy-done.3, f32[128,128]{1,0:T(8,128)S(1)} %copy-done.4, s32[128,128]{1,0:T(8,128)S(1)} %copy-done.5, s32[128,128]{1,0:T(8,128)S(1)} %copy-done.6, f32[256,128]{1,0:T(8,128)S(1)} %bitcast.4, f32[4,12]{1,0:T(4,128)S(1)} %copy-done.10, ...), custom_call_target="tpu_custom_call" | custom-call | tf_op jit(solution)/shard_map/pallas_call | solution.py:312
  34.6 0.7 %copy.17 = f32[2,128,128]{2,1,0:T(8,128)} copy(f32[2,128,128]{2,1,0:T(8,128)S(1)} %get-tuple-element.4) | data formatting | bytes 262144
  35.3 0.7 %copy.18 = f32[8,16,256]{2,1,0:T(8,128)} copy(f32[8,16,256]{2,1,0:T(8,128)S(1)} %get-tuple-element.5) | data formatting | bytes 262144
Async XLA Ops:
  0.6 3.4 %copy-start = (bf16[128,128,256]{2,1,0:T(8,128)(2,1)S(1)}, bf16[128,128,256]{2,1,0:T(8,128)(2,1)}, u32[]{:S(2)}) copy-start(bf16[128,128,256]{2,1,0:T(8,128)(2,1)} %w_hbm.1) | copy-start | bytes 25165828
  4.0 0.9 %copy-start.1 = (f32[32768]{0:T(1024)S(1)}, f32[32768]{0:T(1024)}, u32[]{:S(2)}) copy-start(f32[32768]{0:T(1024)} %param.17) | copy-start | bytes 393220
  4.9 0.9 %copy-start.2 = (f32[8,16,256]{2,1,0:T(8,128)S(1)}, f32[8,16,256]{2,1,0:T(8,128)}, u32[]{:S(2)}) copy-start(f32[8,16,256]{2,1,0:T(8,128)} %param.23) | copy-start | bytes 393220
  5.8 0.8 %copy-start.3 = (f32[128,128]{1,0:T(8,128)S(1)}, f32[128,128]{1,0:T(8,128)}, u32[]{:S(2)}) copy-start(f32[128,128]{1,0:T(8,128)} %wind_hbm.1) | copy-start | bytes 196612
  6.7 0.8 %copy-start.4 = (f32[128,128]{1,0:T(8,128)S(1)}, f32[128,128]{1,0:T(8,128)}, u32[]{:S(2)}) copy-start(f32[128,128]{1,0:T(8,128)} %moist_hbm.1) | copy-start | bytes 196612
  7.5 0.8 %copy-start.5 = (s32[128,128]{1,0:T(8,128)S(1)}, s32[128,128]{1,0:T(8,128)}, u32[]{:S(2)}) copy-start(s32[128,128]{1,0:T(8,128)} %tex_hbm.1) | copy-start | bytes 196612
  8.3 0.8 %copy-start.6 = (s32[128,128]{1,0:T(8,128)S(1)}, s32[128,128]{1,0:T(8,128)}, u32[]{:S(2)}) copy-start(s32[128,128]{1,0:T(8,128)} %index_hbm.1) | copy-start | bytes 196612
  9.2 0.8 %copy-start.7 = (f32[3,16,256]{2,1,0:T(8,128)S(1)}, f32[3,16,256]{2,1,0:T(8,128)}, u32[]{:S(2)}) copy-start(f32[3,16,256]{2,1,0:T(8,128)} %atm_hbm.1) | copy-start | bytes 147460
  10.0 0.7 %copy-start.8 = (f32[4,8,12]{2,1,0:T(8,128)S(1)}, f32[4,8,12]{2,1,0:T(8,128)}, u32[]{:S(2)}) copy-start(f32[4,8,12]{2,1,0:T(8,128)} %blast_hbm.1) | copy-start | bytes 4612
  10.7 0.7 %copy-start.9 = (f32[15,256]{1,0:T(8,128)S(1)}, f32[15,256]{1,0:T(8,128)}, u32[]{:S(2)}) copy-start(f32[15,256]{1,0:T(8,128)} %mix_hbm.1) | copy-start | bytes 46084
  11.4 0.7 %copy-start.10 = (f32[4,12]{1,0:T(4,128)S(1)}, f32[4,12]{1,0:T(4,128)}, u32[]{:S(2)}) copy-start(f32[4,12]{1,0:T(4,128)} %frac_hbm.1) | copy-start | bytes 580
  12.1 0.7 %copy-start.11 = (s32[128,1]{0,1:T(1,128)S(1)}, s32[128,1]{0,1:T(1,128)}, u32[]{:S(2)}) copy-start(s32[128,1]{0,1:T(1,128)} %param.20) | copy-start | bytes 1540
  12.8 0.7 %copy-start.12 = (f32[8]{0:T(128)S(1)}, f32[8]{0:T(128)}, u32[]{:S(2)}) copy-start(f32[8]{0:T(128)} %param.25) | copy-start | bytes 100

commit v2 on v1

--- a/solution.py
+++ b/solution.py
@@ -33,7 +33,7 @@
     w_hbm, atm_hbm, dust_hbm, mix_hbm, settle_hbm,
     land_out, dust_out,
     wind, moist, tex, index, soil, frac, blast, dest_v, dest_s, w, atm, dust, mix, settle,
-    packed, erod, root, coef, part, sums, send, came, mine, gath, numer, base, gain,
+    packed, erod, root, coef, emitted, part, sums, send, came, mine, gath, numer, base, gain,
     in_sem, w_sem, surf_send, surf_recv, flux_send, flux_recv,
 ):
     half = columns // 2
@@ -44,21 +44,30 @@
         copy.start()
         return copy
 
-    c_mix = local(mix_hbm, mix, 0)
-    c_atm = local(atm_hbm, atm, 1)
-    c_map = local(map_hbm, soil, 2)
-    c_index = local(index_hbm, index, 3)
-    c_wind = local(wind_hbm, wind, 4)
-    c_moist = local(moist_hbm, moist, 5)
-    c_tex = local(tex_hbm, tex, 6)
-    c_frac = local(frac_hbm, frac, 7)
-    c_blast = local(blast_hbm, blast, 8)
-    c_dv = local(dest_hbm, dest_v, 9)
-    c_ds = local(dest_hbm, dest_s, 10)
-    c_settle = local(settle_hbm, settle, 11)
-    c_d0 = local(dust_hbm.at[:, 0:half], dust.at[0], 12)
-    c_d1 = local(dust_hbm.at[:, half:columns], dust.at[1], 13)
+    copies = [
+        local(src, dst, k)
+        for k, (src, dst) in enumerate(
+            [
+                (mix_hbm, mix), (atm_hbm, atm), (map_hbm, soil), (index_hbm, index),
+                (dust_hbm.at[:, 0:half], dust.at[0]), (dust_hbm.at[:, half:columns], dust.at[1]),
+                (wind_hbm, wind), (moist_hbm, moist), (tex_hbm, tex), (frac_hbm, frac),
+                (blast_hbm, blast), (dest_hbm, dest_v), (dest_hbm, dest_s), (settle_hbm, settle),
+            ]
+        )
+    ]
     groups = nblocks // 8
+
+    def peer(i):
+        p = lax.rem(me + i, n)
+        return p, (p // nt, lax.rem(p, nt))
+
+    barrier = pltpu.get_barrier_semaphore()
+
+    def greet(i, carry):
+        pl.semaphore_signal(barrier, inc=1, device_id=peer(i)[1], device_id_type=MESH)
+        return carry
+
+    lax.fori_loop(1, n, greet, 0)
 
     def chunk(i):
         at = pl.ds(i * 8, 8)
@@ -69,52 +78,85 @@
         return carry
 
     lax.fori_loop(0, groups, fetch, 0)
-
-    def peer(i):
-        p = lax.rem(me + i, n)
-        return p, (p // nt, lax.rem(p, nt))
-
-    barrier = pltpu.get_barrier_semaphore()
-
-    def greet(i, carry):
-        pl.semaphore_signal(barrier, inc=1, device_id=peer(i)[1], device_id_type=MESH)
-        return carry
-
-    lax.fori_loop(1, n, greet, 0)
-
-    c_mix.wait()
-    c_atm.wait()
+    for copy in copies:
+        copy.wait()
+
+    sink = rows_of([settle[0, f] for f in range(nbins)], (nbins, columns))
     above = None
     held = [None] * 3
+    ratios = [None] * levels
+    values = [None] * levels
     for level in range(levels - 1, -1, -1):
         pivot = jnp.ones((1, columns), F32)
-        low = up = None
+        dust_pivot = jnp.ones((nbins, columns), F32)
+        at = pl.ds(level, nbins, stride=levels)
+        dust_right = jnp.concatenate([dust[0, at, :], dust[1, at, :]], axis=1)
+        low = up = dust_low = None
         if level > 0:
             low = mix[level - 1:level, :]
+            dust_low = jnp.broadcast_to(low, (nbins, columns))
             pivot = pivot + low
+            dust_pivot = dust_pivot + dust_low
         if level < levels - 1:
             up = mix[level:level + 1, :]
             pivot = pivot + up * (1.0 - above)
+            dust_up = jnp.broadcast_to(up, (nbins, columns)) + sink
+            dust_pivot = dust_pivot + dust_up * (1.0 - ratios[level + 1])
+            dust_right = dust_right + dust_up * values[level + 1]
+        else:
+            dust_pivot = dust_pivot + sink
         inverse = 1.0 / pivot
+        dust_inverse = 1.0 / dust_pivot
         for f in range(3):
             right = atm[f, level:level + 1, :]
             if up is not None:
                 right = right + up * held[f]
             held[f] = right * inverse
+        values[level] = dust_right * dust_inverse
         if low is not None:
             above = low * inverse
+            ratios[level] = dust_low * dust_inverse
     speed = jnp.sqrt(held[0] * held[0] + held[1] * held[1] + 0.25)
     mine[0:1, :] = speed.astype(BF16).astype(F32)
     mine[1:2, :] = held[2].astype(BF16).astype(F32)
-
-    c_map.wait()
-    c_index.wait()
+    scale = float(columns) / float(ncells * nblocks)
+    now, step = values[0], dust_inverse * scale
+    base[0], gain[0] = now, step
+    for level in range(1, levels):
+        now = values[level] + ratios[level] * now
+        step = ratios[level] * step
+        base[level], gain[level] = now, step
+
     words = soil.shape[0] // 2
     fixed = jnp.floor(soil[...] * FIXED + 0.5).astype(jnp.int32)
     packed[...] = fixed[:words] + (fixed[words:] << 16)
     bits = words.bit_length() - 1
 
-    def erode(i, carry):
+    coef[...] = jnp.zeros_like(coef)
+    for t in range(ntex):
+        coef[:, 16 * t:16 * t + nsalt] = 40.0 * blast[t] * frac[t:t + 1, :]
+    root[...] = jnp.sqrt(1.0 + 12.1 * moist[...])
+
+    pl.semaphore_wait(barrier, n - 1)
+
+    def send_surface(i, carry):
+        pltpu.make_async_remote_copy(
+            src_ref=mine, dst_ref=gath.at[me], send_sem=surf_send, recv_sem=surf_recv,
+            device_id=peer(i)[1], device_id_type=MESH,
+        ).start()
+        return carry
+
+    lax.fori_loop(1, n, send_surface, 0)
+    gath[me] = mine[...]
+
+    full = coef[:, 0:16 * ntex]
+    coarse = full.astype(BF16)
+    fine = (full - coarse.astype(F32)).astype(BF16)
+    table = jnp.concatenate([coarse, fine], axis=0)
+    thresh0 = rows_of([float(v) for v in threshold_constants(nsalt)], (16, ncells))
+    nothing = jnp.zeros((nbins, ncells), F32)
+
+    def erode(i):
         at = pl.ds(pl.multiple_of(i * 8, 8), 8)
         cell = index[at, :]
         lane = cell & 127
@@ -130,40 +172,8 @@
         word = tree(bits - 1, 0)
         value = jnp.where(row >= words, lax.shift_right_logical(word, 16), word) & 65535
         erod[at, :] = value.astype(F32) * (1.0 / FIXED)
-        return carry
-
-    lax.fori_loop(0, groups, erode, 0)
-
-    pl.semaphore_wait(barrier, n - 1)
-
-    def send_surface(i, carry):
-        pltpu.make_async_remote_copy(
-            src_ref=mine, dst_ref=gath.at[me], send_sem=surf_send, recv_sem=surf_recv,
-            device_id=peer(i)[1], device_id_type=MESH,
-        ).start()
-        return carry
-
-    lax.fori_loop(1, n, send_surface, 0)
-    gath[me] = mine[...]
-
-    c_frac.wait()
-    c_blast.wait()
-    coef[...] = jnp.zeros_like(coef)
-    for t in range(ntex):
-        coef[:, 16 * t:16 * t + nsalt] = 40.0 * blast[t] * frac[t:t + 1, :]
-    full = coef[:, 0:16 * ntex]
-    coarse = full.astype(BF16)
-    fine = (full - coarse.astype(F32)).astype(BF16)
-    table = jnp.concatenate([coarse, fine], axis=0)
-    c_wind.wait()
-    c_moist.wait()
-    c_tex.wait()
-    root[...] = jnp.sqrt(1.0 + 12.1 * moist[...])
-    thresh0 = rows_of([float(v) for v in threshold_constants(nsalt)], (16, ncells))
-    nothing = jnp.zeros((nbins, ncells), F32)
-
-    def regrid(i, carry):
-        chunk(i).wait()
+
+    def emit(i):
         blocks = []
         for j in range(8):
             at = pl.ds(i * 8 + j, 1)
@@ -190,18 +200,38 @@
                     jnp.concatenate([nothing, second], axis=1),
                 ],
                 axis=0,
-            ).astype(BF16)
+            )
+            at = pl.ds(pl.multiple_of((i * 4 + j // 2) * 16, 16), 16)
+            emitted[at, :] = left.astype(BF16)
+
+    def regrid(i):
+        for j in range(0, 8, 2):
+            at = pl.ds(pl.multiple_of((i * 4 + j // 2) * 16, 16), 16)
             weights = w[pl.ds(i * 8 + j, 2)].reshape(2 * ncells, columns)
-            flux = jnp.dot(left, weights, preferred_element_type=F32)
+            flux = jnp.dot(emitted[at, :], weights, preferred_element_type=F32)
             for s in range(2):
                 at = pl.ds(i * 8 + j + s, nbins, stride=nblocks)
                 part[0, at, :] = flux[s * nbins:(s + 1) * nbins, 0:half]
                 part[1, at, :] = flux[s * nbins:(s + 1) * nbins, half:columns]
-        return carry
-
-    lax.fori_loop(0, groups, regrid, 0)
-
-    c_dv.wait()
+
+    erode(0)
+    emit(0)
+    erode(1)
+
+    def steps(i, carry):
+        chunk(i - 2).wait()
+        regrid(i - 2)
+        emit(i - 1)
+        erode(i)
+        return carry
+
+    lax.fori_loop(2, groups, steps, 0)
+    chunk(groups - 2).wait()
+    chunk(groups - 1).wait()
+    regrid(groups - 2)
+    emit(groups - 1)
+    regrid(groups - 1)
+
     tiles = lax.broadcasted_iota(jnp.int32, (n, nblocks), 0)
     placing = jnp.where(jnp.broadcast_to(dest_v[...], (n, nblocks)) == tiles, 1.0, 0.0).astype(BF16)
     placing = jnp.concatenate([placing, placing], axis=1)
@@ -226,46 +256,13 @@
     lax.fori_loop(1, n, send_flux, 0)
     came[me] = send[me]
 
-    c_settle.wait()
-    c_d0.wait()
-    c_d1.wait()
-    sink = rows_of([settle[0, f] for f in range(nbins)], (nbins, columns))
-    ratios = [None] * levels
-    values = [None] * levels
-    for level in range(levels - 1, -1, -1):
-        pivot = jnp.ones((nbins, columns), F32)
-        at = pl.ds(level, nbins, stride=levels)
-        right = jnp.concatenate([dust[0, at, :], dust[1, at, :]], axis=1)
-        low = None
-        if level > 0:
-            low = jnp.broadcast_to(mix[level - 1:level, :], (nbins, columns))
-            pivot = pivot + low
-        if level < levels - 1:
-            up = jnp.broadcast_to(mix[level:level + 1, :], (nbins, columns)) + sink
-            pivot = pivot + up * (1.0 - ratios[level + 1])
-            right = right + up * values[level + 1]
-        else:
-            pivot = pivot + sink
-        inverse = 1.0 / pivot
-        values[level] = right * inverse
-        if low is not None:
-            ratios[level] = low * inverse
-    scale = float(columns) / float(ncells * nblocks)
-    now, step = values[0], inverse * scale
-    base[0], gain[0] = now, step
-    for level in range(1, levels):
-        now = values[level] + ratios[level] * now
-        step = ratios[level] * step
-        base[level], gain[level] = now, step
-
-    c_ds.wait()
     arrived = gath.at[pl.ds(0, n - 1)]
     pltpu.make_async_copy(arrived, arrived, surf_recv).wait()
     rest = jnp.where(lax.broadcasted_iota(jnp.int32, (6, columns), 0) == 0, 1.0, 0.0)
 
     def back(i, carry):
-        for j in range(0, 8, 2):
-            g = i * 8 + j
+        for j in range(0, 16, 2):
+            g = i * 16 + j
             left = jnp.concatenate(
                 [gath[dest_s[0, g]], rest, gath[dest_s[0, g + 1]], rest], axis=0
             ).astype(BF16)
@@ -277,7 +274,7 @@
             numer[pl.ds(pl.multiple_of(g * 8 + 8, 8), 8), :] = found[8:16, ncells:2 * ncells]
         return carry
 
-    lax.fori_loop(0, groups, back, 0)
+    lax.fori_loop(0, groups // 2, back, 0)
     weight = 1.0 / numer[pl.ds(2, nblocks, stride=8), :]
     land_out[0] = numer[pl.ds(0, nblocks, stride=8), :] * weight
     land_out[1] = 0.5 * moist[...] + 0.5 * (numer[pl.ds(1, nblocks, stride=8), :] * weight)
@@ -315,7 +312,7 @@
             jax.ShapeDtypeStruct((2, nblocks, ncells), F32),
             jax.ShapeDtypeStruct((nbins, levels, columns), F32),
         ),
-        in_specs=[pl.BlockSpec(memory_space=pl.ANY)] * 13,
+        in_specs=[pl.BlockSpec(memory_space=pltpu.HBM)] * 13,
         out_specs=(pl.BlockSpec(memory_space=pltpu.VMEM), pl.BlockSpec(memory_space=pltpu.VMEM)),
         scratch_shapes=[
             land,
@@ -336,6 +333,7 @@
             land,
             land,
             pltpu.VMEM((nbins, 128), F32),
+            pltpu.VMEM((nblocks * nbins, columns), BF16),
             pltpu.VMEM((2, nbins * nblocks, half), F32),
             pltpu.VMEM((n * 2 * nbins, half), F32),
             pltpu.VMEM((n, 2 * nbins, half), BF16),
@@ -353,7 +351,7 @@
             pltpu.SemaphoreType.DMA,
         ],
         compiler_params=pltpu.CompilerParams(
-            collective_id=0, has_side_effects=True, vmem_limit_bytes=40 * 1024 * 1024
+            collective_id=0, has_side_effects=True, vmem_limit_bytes=60 * 1024 * 1024
         ),
     )(
         land_wind, land_moist, texture, land_index, soil, mass_frac, blast_table,

time: 36.5 us -> 21.1 us (0.58)
  local copies, waits for them, and re-layouts: 14.1 us -> 3.14 us
  Pallas kernels: 21.2 us -> 17.1 us
    unnamed x28 -> x2, local copies, waits for them, and re-layouts: 14.1 us -> 3.14 us
    pallas_call x1, Pallas kernels: 21.2 us -> 17.1 us  [on_device(): pl.pallas_call(functools.partial(kernel, n, nt, nblocks, ncells, columns,...]
where the time goes in v2:
time: 21.1 us; the launch traced here: 20.9 us
  Pallas kernels  17.1 us (81%)
  local copies, waits for them, and re-layouts  3.14 us (15%)
  between operations  0.64 us (3%)
    pallas_call x1, Pallas kernels, on_device(): pl.pallas_call(functools.partial(kernel, n, nt, nblocks, ncells, columns,...  17.1 us
    unnamed x2, local copies, waits for them, and re-layouts  3.14 us

profile of v2, /device:TPU:0, one launch (start us, length us, event | category | flops | bytes accessed | tf_op | source)
XLA Modules:
  0.0 20.9 jit_solution(15396361137294980722)
XLA Ops:
  0.6 17.1 %shard_map.140 = (f32[2,128,128]{2,1,0:T(8,128)}, f32[8,16,256]{2,1,0:T(8,128)}) custom-call(f32[128,128]{1,0:T(8,128)} %wind_hbm.1, f32[128,128]{1,0:T(8,128)} %moist_hbm.1, s32[128,128]{1,0:T(8,128)} %tex_hbm.1, s32[128,128]{1,0:T(8,128)} %index_hbm.1, f32[256,128]{1,0:T(8,128)} %bitcast.4, f32[4,12]{1,0:T(4,128)} %frac_hbm.1, f32[4,8,12]{2,1,0:T(8,128)} %blast_hbm.1, ...), custom_call_target="tpu_custom_call" | custom-call | tf_op jit(solution)/shard_map/pallas_call | solution.py:309
  17.7 1.6 %copy.17 = f32[2,128,128]{2,1,0:T(8,128)} copy(f32[2,128,128]{2,1,0:T(8,128)} %get-tuple-element.4) | data formatting | bytes 262144
  19.3 1.6 %copy.18 = f32[8,16,256]{2,1,0:T(8,128)} copy(f32[8,16,256]{2,1,0:T(8,128)} %get-tuple-element.5) | data formatting | bytes 262144

commit v3 on v2

--- a/solution.py
+++ b/solution.py
@@ -31,7 +31,7 @@
     n, nt, nblocks, ncells, columns, nbins, nsalt, ntex, levels,
     wind_hbm, moist_hbm, tex_hbm, index_hbm, map_hbm, frac_hbm, blast_hbm, dest_hbm,
     w_hbm, atm_hbm, dust_hbm, mix_hbm, settle_hbm,
-    land_out, dust_out,
+    results,
     wind, moist, tex, index, soil, frac, blast, dest_v, dest_s, w, atm, dust, mix, settle,
     packed, erod, root, coef, emitted, part, sums, send, came, mine, gath, numer, base, gain,
     in_sem, w_sem, surf_send, surf_recv, flux_send, flux_recv,
@@ -276,20 +276,40 @@
 
     lax.fori_loop(0, groups // 2, back, 0)
     weight = 1.0 / numer[pl.ds(2, nblocks, stride=8), :]
-    land_out[0] = numer[pl.ds(0, nblocks, stride=8), :] * weight
-    land_out[1] = 0.5 * moist[...] + 0.5 * (numer[pl.ds(1, nblocks, stride=8), :] * weight)
+    results[0:nblocks, :] = numer[pl.ds(0, nblocks, stride=8), :] * weight
+    results[nblocks:2 * nblocks, :] = 0.5 * moist[...] + 0.5 * (numer[pl.ds(1, nblocks, stride=8), :] * weight)
 
     landed = came.at[pl.ds(0, n - 1)]
     pltpu.make_async_copy(landed, landed, flux_recv).wait()
     flux = jnp.sum(came[...].astype(F32), axis=0)
     flux = jnp.concatenate([flux[0:nbins], flux[nbins:2 * nbins]], axis=1)
     for level in range(levels):
-        dust_out[:, level, :] = base[level] + gain[level] * flux
+        total = base[level] + gain[level] * flux
+        for h in range(2):
+            first = 2 * nblocks + h * nbins * levels + level
+            results[pl.ds(first, nbins, stride=levels), :] = total[:, h * half:(h + 1) * half]
 
     sent = gath.at[pl.ds(0, n - 1)]
     pltpu.make_async_copy(sent, sent, surf_send).wait()
     gone = came.at[pl.ds(0, n - 1)]
     pltpu.make_async_copy(gone, gone, flux_send).wait()
+
+
+def unpack(nblocks, half, results, land_out, dust_out, sem):
+    rows = dust_out.shape[0]
+    copies = [
+        pltpu.make_async_copy(results.at[pl.ds(0, 2 * nblocks)], land_out, sem.at[0]),
+        pltpu.make_async_copy(
+            results.at[pl.ds(2 * nblocks, rows)], dust_out.at[:, 0:half], sem.at[1]
+        ),
+        pltpu.make_async_copy(
+            results.at[pl.ds(2 * nblocks + rows, rows)], dust_out.at[:, half:2 * half], sem.at[2]
+        ),
+    ]
+    for copy in copies:
+        copy.start()
+    for copy in copies:
+        copy.wait()
 
 
 def on_device(
@@ -304,16 +324,18 @@
     n = lax.axis_size(("sec", "tile"))
     groups = nblocks // 8
     soil = erod_map.reshape(-1, 128)
+    operands = (
+        land_wind, land_moist, texture, land_index, soil, mass_frac, blast_table,
+        dest_tile.reshape(1, nblocks), regrid_w, atm_state,
+        dust_mix.reshape(nbins * levels, columns), mixing, settle.reshape(1, nbins),
+    )
     land = pltpu.VMEM((nblocks, ncells), F32)
     whole = pltpu.VMEM((nblocks, ncells), jnp.int32)
-    return pl.pallas_call(
+    results = pl.pallas_call(
         functools.partial(kernel, n, nt, nblocks, ncells, columns, nbins, nsalt, ntex, levels),
-        out_shape=(
-            jax.ShapeDtypeStruct((2, nblocks, ncells), F32),
-            jax.ShapeDtypeStruct((nbins, levels, columns), F32),
-        ),
+        out_shape=jax.ShapeDtypeStruct((2 * nblocks + 2 * nbins * levels, 128), F32),
         in_specs=[pl.BlockSpec(memory_space=pltpu.HBM)] * 13,
-        out_specs=(pl.BlockSpec(memory_space=pltpu.VMEM), pl.BlockSpec(memory_space=pltpu.VMEM)),
+        out_specs=pl.BlockSpec(memory_space=pltpu.VMEM),
         scratch_shapes=[
             land,
             land,
@@ -351,13 +373,20 @@
             pltpu.SemaphoreType.DMA,
         ],
         compiler_params=pltpu.CompilerParams(
-            collective_id=0, has_side_effects=True, vmem_limit_bytes=60 * 1024 * 1024
+            collective_id=0, has_side_effects=True, vmem_limit_bytes=40 * 1024 * 1024
         ),
-    )(
-        land_wind, land_moist, texture, land_index, soil, mass_frac, blast_table,
-        dest_tile.reshape(1, nblocks), regrid_w, atm_state,
-        dust_mix.reshape(nbins * levels, columns), mixing, settle.reshape(1, nbins),
-    )
+    )(*(pltpu.with_memory_space_constraint(x, pltpu.HBM) for x in operands))
+    land_out, dust_out = pl.pallas_call(
+        functools.partial(unpack, nblocks, half),
+        out_shape=(
+            jax.ShapeDtypeStruct((2 * nblocks, ncells), F32),
+            jax.ShapeDtypeStruct((nbins * levels, columns), F32),
+        ),
+        in_specs=[pl.BlockSpec(memory_space=pl.ANY)],
+        out_specs=(pl.BlockSpec(memory_space=pltpu.HBM), pl.BlockSpec(memory_space=pltpu.HBM)),
+        scratch_shapes=[pltpu.SemaphoreType.DMA((3,))],
+    )(results)
+    return land_out.reshape(2, nblocks, ncells), dust_out.reshape(nbins, levels, columns)
 
 
 def solution(mesh):

time: 21.1 us -> 27 us (1.28)
  Pallas kernels: 17.1 us -> 25.5 us
  local copies, waits for them, and re-layouts: 3.14 us -> 0.68 us
    pallas_call x0 -> x1, Pallas kernels: none -> 9.07 us  [on_device(): pl.pallas_call(functools.partial(unpack, nblocks, half), out_shape=(jax.S...]
    unnamed x2, local copies, waits for them, and re-layouts: 3.14 us -> 0.68 us
    pallas_call x1, Pallas kernels: 17.1 us -> 16.4 us  [on_device(): pl.pallas_call(functools.partial(kernel, n, nt, nblocks, ncells, columns,...]
where the time goes in v3:
time: 27 us; the launch traced here: 26.8 us
  Pallas kernels  25.5 us (94%)
  local copies, waits for them, and re-layouts  0.68 us (3%)
  between operations  0.65 us (2%)
    pallas_call x1, Pallas kernels, on_device(): pl.pallas_call(functools.partial(kernel, n, nt, nblocks, ncells, columns,...  16.4 us
    pallas_call x1, Pallas kernels, on_device(): pl.pallas_call(functools.partial(unpack, nblocks, half), out_shape=(jax.S...  9.07 us
    unnamed x2, local copies, waits for them, and re-layouts  0.68 us

profile of v3, /device:TPU:0, one launch (start us, length us, event | category | flops | bytes accessed | tf_op | source)
XLA Modules:
  0.0 26.8 jit_solution(5055157755083376983)
XLA Ops:
  0.6 16.4 %shard_map.140.results = f32[512,128]{1,0:T(8,128)S(1)} custom-call(f32[128,128]{1,0:T(8,128)} %wind_hbm.1, f32[128,128]{1,0:T(8,128)} %moist_hbm.1, s32[128,128]{1,0:T(8,128)} %tex_hbm.1, s32[128,128]{1,0:T(8,128)} %index_hbm.1, f32[256,128]{1,0:T(8,128)} %bitcast.6, f32[4,12]{1,0:T(4,128)} %frac_hbm.1, f32[4,8,12]{2,1,0:T(8,128)} %blast_hbm.1, ...), custom_call_target="tpu_custom_call" | custom-call | tf_op jit(solution)/shard_map/pallas_call | solution.py:334
  17.0 0.0 copy-start
  17.1 0.7 %copy-done = f32[512,128]{1,0:T(8,128)} copy-done((f32[512,128]{1,0:T(8,128)}, f32[512,128]{1,0:T(8,128)S(1)}, u32[]{:S(2)}) %copy-start) | copy-done | bytes 262168
  17.7 9.1 %shard_map.141 = (f32[256,128]{1,0:T(8,128)}, f32[128,256]{1,0:T(8,128)}) custom-call(f32[512,128]{1,0:T(8,128)} %copy-done), custom_call_target="tpu_custom_call" | custom-call | tf_op jit(solution)/shard_map/pallas_call | solution.py:379
Async XLA Ops:
  17.0 0.7 %copy-start = (f32[512,128]{1,0:T(8,128)}, f32[512,128]{1,0:T(8,128)S(1)}, u32[]{:S(2)}) copy-start(f32[512,128]{1,0:T(8,128)S(1)} %shard_map.140.results) | copy-start | bytes 786436

commit v4 on v3

--- a/solution.py
+++ b/solution.py
@@ -8,7 +8,8 @@
 from jax.experimental.pallas import tpu as pltpu
 from jax.sharding import PartitionSpec as P
 
-MESH = pl.DeviceIdType.MESH
+FLAT = pl.DeviceIdType.LOGICAL
+STEP = 4
 F32 = jnp.float32
 BF16 = jnp.bfloat16
 FIXED = 65535.0
@@ -57,17 +58,26 @@
     ]
     groups = nblocks // 8
 
-    def peer(i):
-        p = lax.rem(me + i, n)
-        return p, (p // nt, lax.rem(p, nt))
+    def each_peer(act):
+        def several(i, carry):
+            for j in range(STEP):
+                one(i * STEP + j + 1)
+            return carry
+
+        def one(i):
+            p = me + i
+            act(jnp.where(p >= n, p - n, p))
+
+        lax.fori_loop(0, (n - 1) // STEP, several, 0)
+        for i in range((n - 1) // STEP * STEP + 1, n):
+            one(i)
 
     barrier = pltpu.get_barrier_semaphore()
 
-    def greet(i, carry):
-        pl.semaphore_signal(barrier, inc=1, device_id=peer(i)[1], device_id_type=MESH)
-        return carry
-
-    lax.fori_loop(1, n, greet, 0)
+    def greet(p):
+        pl.semaphore_signal(barrier, inc=1, device_id=p, device_id_type=FLAT)
+
+    each_peer(greet)
 
     def chunk(i):
         at = pl.ds(i * 8, 8)
@@ -137,18 +147,6 @@
         coef[:, 16 * t:16 * t + nsalt] = 40.0 * blast[t] * frac[t:t + 1, :]
     root[...] = jnp.sqrt(1.0 + 12.1 * moist[...])
 
-    pl.semaphore_wait(barrier, n - 1)
-
-    def send_surface(i, carry):
-        pltpu.make_async_remote_copy(
-            src_ref=mine, dst_ref=gath.at[me], send_sem=surf_send, recv_sem=surf_recv,
-            device_id=peer(i)[1], device_id_type=MESH,
-        ).start()
-        return carry
-
-    lax.fori_loop(1, n, send_surface, 0)
-    gath[me] = mine[...]
-
     full = coef[:, 0:16 * ntex]
     coarse = full.astype(BF16)
     fine = (full - coarse.astype(F32)).astype(BF16)
@@ -218,6 +216,17 @@
     emit(0)
     erode(1)
 
+    pl.semaphore_wait(barrier, n - 1)
+
+    def send_surface(p):
+        pltpu.make_async_remote_copy(
+            src_ref=mine, dst_ref=gath.at[me], send_sem=surf_send, recv_sem=surf_recv,
+            device_id=p, device_id_type=FLAT,
+        ).start()
+
+    each_peer(send_surface)
+    gath[me] = mine[...]
+
     def steps(i, carry):
         chunk(i - 2).wait()
         regrid(i - 2)
@@ -245,15 +254,13 @@
         sums[pl.ds(nbins + k, n, stride=2 * nbins), :] = total[:, half:columns]
     send[...] = sums[...].reshape(n, 2 * nbins, half).astype(BF16)
 
-    def send_flux(i, carry):
-        p, target = peer(i)
+    def send_flux(p):
         pltpu.make_async_remote_copy(
             src_ref=send.at[p], dst_ref=came.at[me], send_sem=flux_send, recv_sem=flux_recv,
-            device_id=target, device_id_type=MESH,
+            device_id=p, device_id_type=FLAT,
         ).start()
-        return carry
-
-    lax.fori_loop(1, n, send_flux, 0)
+
+    each_peer(send_flux)
     came[me] = send[me]
 
     arrived = gath.at[pl.ds(0, n - 1)]
@@ -382,10 +389,11 @@
             jax.ShapeDtypeStruct((2 * nblocks, ncells), F32),
             jax.ShapeDtypeStruct((nbins * levels, columns), F32),
         ),
-        in_specs=[pl.BlockSpec(memory_space=pl.ANY)],
+        in_specs=[pl.BlockSpec(memory_space=pltpu.VMEM)],
         out_specs=(pl.BlockSpec(memory_space=pltpu.HBM), pl.BlockSpec(memory_space=pltpu.HBM)),
         scratch_shapes=[pltpu.SemaphoreType.DMA((3,))],
-    )(results)
+        compiler_params=pltpu.CompilerParams(vmem_limit_bytes=16 * 1024 * 1024),
+    )(pltpu.with_memory_space_constraint(results, pltpu.VMEM))
     return land_out.reshape(2, nblocks, ncells), dust_out.reshape(nbins, levels, columns)
 
 

time: 27 us -> 17.3 us (0.64)
  Pallas kernels: 25.5 us -> 16.4 us
  local copies, waits for them, and re-layouts: 0.68 us -> 0 us
    pallas_call x1, Pallas kernels: 9.07 us -> 0.72 us  [on_device(): pl.pallas_call(functools.partial(unpack, nblocks, half), out_shape=(jax.S...]
    pallas_call x1, Pallas kernels: 16.4 us -> 15.6 us  [on_device(): pl.pallas_call(functools.partial(kernel, n, nt, nblocks, ncells, columns,...]
    unnamed x2 -> x0, local copies, waits for them, and re-layouts: 0.68 us -> none
where the time goes in v4:
time: 17.3 us; the launch traced here: 17 us
  Pallas kernels  16.4 us (95%)
  between operations  0.64 us (4%)
    pallas_call x1, Pallas kernels, on_device(): pl.pallas_call(functools.partial(kernel, n, nt, nblocks, ncells, columns,...  15.6 us
    pallas_call x1, Pallas kernels, on_device(): pl.pallas_call(functools.partial(unpack, nblocks, half), out_shape=(jax.S...  0.72 us

profile of v4, /device:TPU:0, one launch (start us, length us, event | category | flops | bytes accessed | tf_op | source)
XLA Modules:
  0.0 17.0 jit_solution(5024762793053105167)
XLA Ops:
  0.6 15.6 %shard_map.140.results = f32[512,128]{1,0:T(8,128)S(1)} custom-call(f32[128,128]{1,0:T(8,128)} %wind_hbm.1, f32[128,128]{1,0:T(8,128)} %moist_hbm.1, s32[128,128]{1,0:T(8,128)} %tex_hbm.1, s32[128,128]{1,0:T(8,128)} %index_hbm.1, f32[256,128]{1,0:T(8,128)} %bitcast.6, f32[4,12]{1,0:T(4,128)} %frac_hbm.1, f32[4,8,12]{2,1,0:T(8,128)} %blast_hbm.1, ...), custom_call_target="tpu_custom_call" | custom-call | tf_op jit(solution)/shard_map/pallas_call | solution.py:341
  16.3 0.7 %shard_map.141 = (f32[256,128]{1,0:T(8,128)}, f32[128,256]{1,0:T(8,128)}) custom-call(f32[512,128]{1,0:T(8,128)S(1)} %shard_map.140.results), custom_call_target="tpu_custom_call" | custom-call | tf_op jit(solution)/shard_map/pallas_call | solution.py:386

commit v5 on v4

--- a/solution.py
+++ b/solution.py
@@ -10,6 +10,7 @@
 
 FLAT = pl.DeviceIdType.LOGICAL
 STEP = 4
+GROUP = 16
 F32 = jnp.float32
 BF16 = jnp.bfloat16
 FIXED = 65535.0
@@ -49,14 +50,25 @@
         local(src, dst, k)
         for k, (src, dst) in enumerate(
             [
-                (mix_hbm, mix), (atm_hbm, atm), (map_hbm, soil), (index_hbm, index),
-                (dust_hbm.at[:, 0:half], dust.at[0]), (dust_hbm.at[:, half:columns], dust.at[1]),
+                (map_hbm, soil), (index_hbm, index), (mix_hbm, mix), (atm_hbm, atm),
                 (wind_hbm, wind), (moist_hbm, moist), (tex_hbm, tex), (frac_hbm, frac),
                 (blast_hbm, blast), (dest_hbm, dest_v), (dest_hbm, dest_s), (settle_hbm, settle),
+                (dust_hbm.at[:, 0:half], dust.at[0]), (dust_hbm.at[:, half:columns], dust.at[1]),
             ]
         )
     ]
-    groups = nblocks // 8
+    groups = nblocks // GROUP
+
+    def chunk(i):
+        at = pl.ds(i * GROUP, GROUP)
+        return pltpu.make_async_copy(w_hbm.at[at], w.at[at], w_sem.at[i])
+
+    for i in range(groups):
+        chunk(i).start()
+
+    def turned(i):
+        p = me + i
+        return jnp.where(p >= n, p - n, p)
 
     def each_peer(act):
         def several(i, carry):
@@ -65,8 +77,7 @@
             return carry
 
         def one(i):
-            p = me + i
-            act(jnp.where(p >= n, p - n, p))
+            act(turned(i))
 
         lax.fori_loop(0, (n - 1) // STEP, several, 0)
         for i in range((n - 1) // STEP * STEP + 1, n):
@@ -79,63 +90,31 @@
 
     each_peer(greet)
 
-    def chunk(i):
-        at = pl.ds(i * 8, 8)
-        return pltpu.make_async_copy(w_hbm.at[at], w.at[at], w_sem.at[i])
-
-    def fetch(i, carry):
-        chunk(i).start()
-        return carry
-
-    lax.fori_loop(0, groups, fetch, 0)
-    for copy in copies:
+    for copy in copies[:10]:
         copy.wait()
 
-    sink = rows_of([settle[0, f] for f in range(nbins)], (nbins, columns))
     above = None
     held = [None] * 3
-    ratios = [None] * levels
-    values = [None] * levels
     for level in range(levels - 1, -1, -1):
         pivot = jnp.ones((1, columns), F32)
-        dust_pivot = jnp.ones((nbins, columns), F32)
-        at = pl.ds(level, nbins, stride=levels)
-        dust_right = jnp.concatenate([dust[0, at, :], dust[1, at, :]], axis=1)
-        low = up = dust_low = None
+        low = up = None
         if level > 0:
             low = mix[level - 1:level, :]
-            dust_low = jnp.broadcast_to(low, (nbins, columns))
             pivot = pivot + low
-            dust_pivot = dust_pivot + dust_low
         if level < levels - 1:
             up = mix[level:level + 1, :]
             pivot = pivot + up * (1.0 - above)
-            dust_up = jnp.broadcast_to(up, (nbins, columns)) + sink
-            dust_pivot = dust_pivot + dust_up * (1.0 - ratios[level + 1])
-            dust_right = dust_right + dust_up * values[level + 1]
-        else:
-            dust_pivot = dust_pivot + sink
         inverse = 1.0 / pivot
-        dust_inverse = 1.0 / dust_pivot
         for f in range(3):
             right = atm[f, level:level + 1, :]
             if up is not None:
                 right = right + up * held[f]
             held[f] = right * inverse
-        values[level] = dust_right * dust_inverse
         if low is not None:
             above = low * inverse
-            ratios[level] = dust_low * dust_inverse
     speed = jnp.sqrt(held[0] * held[0] + held[1] * held[1] + 0.25)
     mine[0:1, :] = speed.astype(BF16).astype(F32)
     mine[1:2, :] = held[2].astype(BF16).astype(F32)
-    scale = float(columns) / float(ncells * nblocks)
-    now, step = values[0], dust_inverse * scale
-    base[0], gain[0] = now, step
-    for level in range(1, levels):
-        now = values[level] + ratios[level] * now
-        step = ratios[level] * step
-        base[level], gain[level] = now, step
 
     words = soil.shape[0] // 2
     fixed = jnp.floor(soil[...] * FIXED + 0.5).astype(jnp.int32)
@@ -155,6 +134,10 @@
     nothing = jnp.zeros((nbins, ncells), F32)
 
     def erode(i):
+        for j in range(GROUP // 8):
+            erode_rows(i * (GROUP // 8) + j)
+
+    def erode_rows(i):
         at = pl.ds(pl.multiple_of(i * 8, 8), 8)
         cell = index[at, :]
         lane = cell & 127
@@ -173,8 +156,8 @@
 
     def emit(i):
         blocks = []
-        for j in range(8):
-            at = pl.ds(i * 8 + j, 1)
+        for j in range(GROUP):
+            at = pl.ds(i * GROUP + j, 1)
             speed_row = jnp.broadcast_to(wind[at, :], (16, ncells))
             thresh = thresh0 * jnp.broadcast_to(root[at, :], (16, ncells))
             total = speed_row + thresh
@@ -189,7 +172,7 @@
             )
         both = jnp.dot(table, jnp.concatenate(blocks, axis=1), preferred_element_type=F32)
         emission = both[0:nbins] + both[nbins:2 * nbins]
-        for j in range(0, 8, 2):
+        for j in range(0, GROUP, 2):
             first = emission[:, j * ncells:(j + 1) * ncells]
             second = emission[:, (j + 1) * ncells:(j + 2) * ncells]
             left = jnp.concatenate(
@@ -199,16 +182,16 @@
                 ],
                 axis=0,
             )
-            at = pl.ds(pl.multiple_of((i * 4 + j // 2) * 16, 16), 16)
+            at = pl.ds(pl.multiple_of((i * (GROUP // 2) + j // 2) * 16, 16), 16)
             emitted[at, :] = left.astype(BF16)
 
     def regrid(i):
-        for j in range(0, 8, 2):
-            at = pl.ds(pl.multiple_of((i * 4 + j // 2) * 16, 16), 16)
-            weights = w[pl.ds(i * 8 + j, 2)].reshape(2 * ncells, columns)
+        for j in range(0, GROUP, 2):
+            at = pl.ds(pl.multiple_of((i * (GROUP // 2) + j // 2) * 16, 16), 16)
+            weights = w[pl.ds(i * GROUP + j, 2)].reshape(2 * ncells, columns)
             flux = jnp.dot(emitted[at, :], weights, preferred_element_type=F32)
             for s in range(2):
-                at = pl.ds(i * 8 + j + s, nbins, stride=nblocks)
+                at = pl.ds(i * GROUP + j + s, nbins, stride=nblocks)
                 part[0, at, :] = flux[s * nbins:(s + 1) * nbins, 0:half]
                 part[1, at, :] = flux[s * nbins:(s + 1) * nbins, half:columns]
 
@@ -224,10 +207,14 @@
             device_id=p, device_id_type=FLAT,
         ).start()
 
-    each_peer(send_surface)
     gath[me] = mine[...]
+    share = (n - 1) // (groups - 2)
+    for i in range(share * (groups - 2) + 1, n):
+        send_surface(turned(i))
 
     def steps(i, carry):
+        for j in range(share):
+            send_surface(turned((i - 2) * share + j + 1))
         chunk(i - 2).wait()
         regrid(i - 2)
         emit(i - 1)
@@ -263,13 +250,44 @@
     each_peer(send_flux)
     came[me] = send[me]
 
+    for copy in copies[10:]:
+        copy.wait()
+    sink = rows_of([settle[0, f] for f in range(nbins)], (nbins, columns))
+    ratios = [None] * levels
+    values = [None] * levels
+    for level in range(levels - 1, -1, -1):
+        pivot = jnp.ones((nbins, columns), F32)
+        at = pl.ds(level, nbins, stride=levels)
+        right = jnp.concatenate([dust[0, at, :], dust[1, at, :]], axis=1)
+        low = None
+        if level > 0:
+            low = jnp.broadcast_to(mix[level - 1:level, :], (nbins, columns))
+            pivot = pivot + low
+        if level < levels - 1:
+            up = jnp.broadcast_to(mix[level:level + 1, :], (nbins, columns)) + sink
+            pivot = pivot + up * (1.0 - ratios[level + 1])
+            right = right + up * values[level + 1]
+        else:
+            pivot = pivot + sink
+        inverse = 1.0 / pivot
+        values[level] = right * inverse
+        if low is not None:
+            ratios[level] = low * inverse
+    scale = float(columns) / float(ncells * nblocks)
+    now, step = values[0], inverse * scale
+    base[0], gain[0] = now, step
+    for level in range(1, levels):
+        now = values[level] + ratios[level] * now
+        step = ratios[level] * step
+        base[level], gain[level] = now, step
+
     arrived = gath.at[pl.ds(0, n - 1)]
     pltpu.make_async_copy(arrived, arrived, surf_recv).wait()
     rest = jnp.where(lax.broadcasted_iota(jnp.int32, (6, columns), 0) == 0, 1.0, 0.0)
 
     def back(i, carry):
-        for j in range(0, 16, 2):
-            g = i * 16 + j
+        for j in range(0, GROUP, 2):
+            g = i * GROUP + j
             left = jnp.concatenate(
                 [gath[dest_s[0, g]], rest, gath[dest_s[0, g + 1]], rest], axis=0
             ).astype(BF16)
@@ -281,7 +299,7 @@
             numer[pl.ds(pl.multiple_of(g * 8 + 8, 8), 8), :] = found[8:16, ncells:2 * ncells]
         return carry
 
-    lax.fori_loop(0, groups // 2, back, 0)
+    lax.fori_loop(0, groups, back, 0)
     weight = 1.0 / numer[pl.ds(2, nblocks, stride=8), :]
     results[0:nblocks, :] = numer[pl.ds(0, nblocks, stride=8), :] * weight
     results[nblocks:2 * nblocks, :] = 0.5 * moist[...] + 0.5 * (numer[pl.ds(1, nblocks, stride=8), :] * weight)
@@ -329,7 +347,7 @@
     levels = atm_state.shape[1]
     half = columns // 2
     n = lax.axis_size(("sec", "tile"))
-    groups = nblocks // 8
+    groups = nblocks // GROUP
     soil = erod_map.reshape(-1, 128)
     operands = (
         land_wind, land_moist, texture, land_index, soil, mass_frac, blast_table,

time: 17.3 us -> 17.5 us (1.012)
  Pallas kernels: 16.4 us -> 16.7 us
    pallas_call x1, Pallas kernels: 15.6 us -> 16 us  [on_device(): pl.pallas_call(functools.partial(kernel, n, nt, nblocks, ncells, columns,...]
where the time goes in v5:
time: 17.5 us; the launch traced here: 17.3 us
  Pallas kernels  16.7 us (95%)
  between operations  0.64 us (4%)
    pallas_call x1, Pallas kernels, on_device(): pl.pallas_call(functools.partial(kernel, n, nt, nblocks, ncells, columns,...  16 us
    pallas_call x1, Pallas kernels, on_device(): pl.pallas_call(functools.partial(unpack, nblocks, half), out_shape=(jax.S...  0.72 us

profile of v5, /device:TPU:0, one launch (start us, length us, event | category | flops | bytes accessed | tf_op | source)
XLA Modules:
  0.0 17.3 jit_solution(307766369915438900)
XLA Ops:
  0.6 16.0 %shard_map.140.results = f32[512,128]{1,0:T(8,128)S(1)} custom-call(f32[128,128]{1,0:T(8,128)} %wind_hbm.1, f32[128,128]{1,0:T(8,128)} %moist_hbm.1, s32[128,128]{1,0:T(8,128)} %tex_hbm.1, s32[128,128]{1,0:T(8,128)} %index_hbm.1, f32[256,128]{1,0:T(8,128)} %bitcast.6, f32[4,12]{1,0:T(4,128)} %frac_hbm.1, f32[4,8,12]{2,1,0:T(8,128)} %blast_hbm.1, ...), custom_call_target="tpu_custom_call" | custom-call | tf_op jit(solution)/shard_map/pallas_call | solution.py:359
  16.6 0.7 %shard_map.141 = (f32[256,128]{1,0:T(8,128)}, f32[128,256]{1,0:T(8,128)}) custom-call(f32[512,128]{1,0:T(8,128)S(1)} %shard_map.140.results), custom_call_target="tpu_custom_call" | custom-call | tf_op jit(solution)/shard_map/pallas_call | solution.py:404

commit v6 on v5

--- a/solution.py
+++ b/solution.py
@@ -35,7 +35,7 @@
     w_hbm, atm_hbm, dust_hbm, mix_hbm, settle_hbm,
     results,
     wind, moist, tex, index, soil, frac, blast, dest_v, dest_s, w, atm, dust, mix, settle,
-    packed, erod, root, coef, emitted, part, sums, send, came, mine, gath, numer, base, gain,
+    packed, erod, root, coef, emitted, part, sums, send, came, mine, gath, picked, numer, base, gain,
     in_sem, w_sem, surf_send, surf_recv, flux_send, flux_recv,
 ):
     half = columns // 2
@@ -283,26 +283,30 @@
 
     arrived = gath.at[pl.ds(0, n - 1)]
     pltpu.make_async_copy(arrived, arrived, surf_recv).wait()
-    rest = jnp.where(lax.broadcasted_iota(jnp.int32, (6, columns), 0) == 0, 1.0, 0.0)
-
-    def back(i, carry):
-        for j in range(0, GROUP, 2):
-            g = i * GROUP + j
-            left = jnp.concatenate(
-                [gath[dest_s[0, g]], rest, gath[dest_s[0, g + 1]], rest], axis=0
-            ).astype(BF16)
-            weights = w[pl.ds(g, 2)].reshape(2 * ncells, columns)
-            found = lax.dot_general(
-                left, weights, (((1,), (1,)), ((), ())), preferred_element_type=F32
-            )
-            numer[pl.ds(pl.multiple_of(g * 8, 8), 8), :] = found[0:8, 0:ncells]
-            numer[pl.ds(pl.multiple_of(g * 8 + 8, 8), 8), :] = found[8:16, ncells:2 * ncells]
+    picked[...] = jnp.where(
+        lax.broadcasted_iota(jnp.int32, picked.shape, 0) % 4 == 2, 1.0, 0.0
+    )
+    owner = lax.broadcasted_iota(jnp.int32, (ncells, 128), 1) // 4
+
+    def back(q, carry):
+        for j in range(32):
+            picked[4 * j:4 * j + 2, :] = gath[dest_s[0, q * 32 + j]]
+        across = picked[...].T.astype(BF16)
+        found = jnp.zeros((ncells, 128), F32)
+        for j in range(0, 32, 8):
+            rows = w[pl.ds(q * 32 + j, 8)].reshape(8 * ncells, columns)
+            product = jnp.dot(rows, across, preferred_element_type=F32)
+            for s in range(8):
+                found = jnp.where(owner == j + s, product[s * ncells:(s + 1) * ncells], found)
+        numer[pl.ds(pl.multiple_of(q * 128, 128), 128), :] = found.T
         return carry
 
-    lax.fori_loop(0, groups, back, 0)
-    weight = 1.0 / numer[pl.ds(2, nblocks, stride=8), :]
-    results[0:nblocks, :] = numer[pl.ds(0, nblocks, stride=8), :] * weight
-    results[nblocks:2 * nblocks, :] = 0.5 * moist[...] + 0.5 * (numer[pl.ds(1, nblocks, stride=8), :] * weight)
+    lax.fori_loop(0, nblocks // 32, back, 0)
+    weight = 1.0 / numer[pl.ds(2, nblocks, stride=4), :]
+    results[0:nblocks, :] = numer[pl.ds(0, nblocks, stride=4), :] * weight
+    results[nblocks:2 * nblocks, :] = (
+        0.5 * moist[...] + 0.5 * (numer[pl.ds(1, nblocks, stride=4), :] * weight)
+    )
 
     landed = came.at[pl.ds(0, n - 1)]
     pltpu.make_async_copy(landed, landed, flux_recv).wait()
@@ -387,7 +391,8 @@
             pltpu.VMEM((n, 2 * nbins, half), BF16),
             pltpu.VMEM((2, columns), F32),
             pltpu.VMEM((n, 2, columns), F32),
-            pltpu.VMEM((nblocks * 8, ncells), F32),
+            pltpu.VMEM((128, columns), F32),
+            pltpu.VMEM((nblocks * 4, ncells), F32),
             pltpu.VMEM((levels, nbins, columns), F32),
             pltpu.VMEM((levels, nbins, columns), F32),
             pltpu.SemaphoreType.DMA((14,)),

time: 17.5 us -> 17.9 us (1.023)
  Pallas kernels: 16.7 us -> 17.1 us
    pallas_call x1, Pallas kernels: 16 us -> 16.4 us  [on_device(): pl.pallas_call(functools.partial(kernel, n, nt, nblocks, ncells, columns,...]
where the time goes in v6:
time: 17.9 us; the launch traced here: 17.8 us
  Pallas kernels  17.1 us (96%)
  between operations  0.64 us (4%)
    pallas_call x1, Pallas kernels, on_device(): pl.pallas_call(functools.partial(kernel, n, nt, nblocks, ncells, columns,...  16.4 us
    pallas_call x1, Pallas kernels, on_device(): pl.pallas_call(functools.partial(unpack, nblocks, half), out_shape=(jax.S...  0.72 us

profile of v6, /device:TPU:0, one launch (start us, length us, event | category | flops | bytes accessed | tf_op | source)
XLA Modules:
  0.0 17.8 jit_solution(15026140696462421702)
XLA Ops:
  0.6 16.4 %shard_map.140.results = f32[512,128]{1,0:T(8,128)S(1)} custom-call(f32[128,128]{1,0:T(8,128)} %wind_hbm.1, f32[128,128]{1,0:T(8,128)} %moist_hbm.1, s32[128,128]{1,0:T(8,128)} %tex_hbm.1, s32[128,128]{1,0:T(8,128)} %index_hbm.1, f32[256,128]{1,0:T(8,128)} %bitcast.6, f32[4,12]{1,0:T(4,128)} %frac_hbm.1, f32[4,8,12]{2,1,0:T(8,128)} %blast_hbm.1, ...), custom_call_target="tpu_custom_call" | custom-call | tf_op jit(solution)/shard_map/pallas_call | solution.py:363
  17.1 0.7 %shard_map.141 = (f32[256,128]{1,0:T(8,128)}, f32[128,256]{1,0:T(8,128)}) custom-call(f32[512,128]{1,0:T(8,128)S(1)} %shard_map.140.results), custom_call_target="tpu_custom_call" | custom-call | tf_op jit(solution)/shard_map/pallas_call | solution.py:409

commit v7 on v5

--- a/solution.py
+++ b/solution.py
@@ -199,6 +199,16 @@
     emit(0)
     erode(1)
 
+    def steps(i, carry):
+        chunk(i - 2).wait()
+        regrid(i - 2)
+        emit(i - 1)
+        erode(i)
+        return carry
+
+    middle = (groups + 2) // 2
+    lax.fori_loop(2, middle, steps, 0)
+
     pl.semaphore_wait(barrier, n - 1)
 
     def send_surface(p):
@@ -207,21 +217,9 @@
             device_id=p, device_id_type=FLAT,
         ).start()
 
+    each_peer(send_surface)
     gath[me] = mine[...]
-    share = (n - 1) // (groups - 2)
-    for i in range(share * (groups - 2) + 1, n):
-        send_surface(turned(i))
-
-    def steps(i, carry):
-        for j in range(share):
-            send_surface(turned((i - 2) * share + j + 1))
-        chunk(i - 2).wait()
-        regrid(i - 2)
-        emit(i - 1)
-        erode(i)
-        return carry
-
-    lax.fori_loop(2, groups, steps, 0)
+    lax.fori_loop(middle, groups, steps, 0)
     chunk(groups - 2).wait()
     chunk(groups - 1).wait()
     regrid(groups - 2)

time: 17.5 us -> 17.5 us (level)
  no operation moved by 1% of the time
where the time goes in v7:
time: 17.5 us; the launch traced here: 17.4 us
  Pallas kernels  16.7 us (95%)
  between operations  0.64 us (4%)
    pallas_call x1, Pallas kernels, on_device(): pl.pallas_call(functools.partial(kernel, n, nt, nblocks, ncells, columns,...  16 us
    pallas_call x1, Pallas kernels, on_device(): pl.pallas_call(functools.partial(unpack, nblocks, half), out_shape=(jax.S...  0.72 us

profile of v7, /device:TPU:0, one launch (start us, length us, event | category | flops | bytes accessed | tf_op | source)
XLA Modules:
  0.0 17.4 jit_solution(3417941801175574760)
XLA Ops:
  0.6 16.0 %shard_map.140.results = f32[512,128]{1,0:T(8,128)S(1)} custom-call(f32[128,128]{1,0:T(8,128)} %wind_hbm.1, f32[128,128]{1,0:T(8,128)} %moist_hbm.1, s32[128,128]{1,0:T(8,128)} %tex_hbm.1, s32[128,128]{1,0:T(8,128)} %index_hbm.1, f32[256,128]{1,0:T(8,128)} %bitcast.6, f32[4,12]{1,0:T(4,128)} %frac_hbm.1, f32[4,8,12]{2,1,0:T(8,128)} %blast_hbm.1, ...), custom_call_target="tpu_custom_call" | custom-call | tf_op jit(solution)/shard_map/pallas_call | solution.py:357
  16.6 0.7 %shard_map.141 = (f32[256,128]{1,0:T(8,128)}, f32[128,256]{1,0:T(8,128)}) custom-call(f32[512,128]{1,0:T(8,128)S(1)} %shard_map.140.results), custom_call_target="tpu_custom_call" | custom-call | tf_op jit(solution)/shard_map/pallas_call | solution.py:402
